TPU v7x, 128 devices: a whole 4x4x4 slice. The times are simulated.
128 devices in a mesh: dp: 16 (over x_lo, z, core), tensor: 8 (over x_hi, y).
Axes of the slice: x: 4 (x_hi: 2, x_lo: 2; x = x_hi * 2 + x_lo), y: 4, z: 4, core: 2. Of those that a mesh axis runs over, the one named last changes fastest.
Arguments:
- tokens: bfloat16 [16384, 1024], P(('dp', 'tensor')), may hold values from -6 to 6
- lengths: int32 [16, 4], P('dp'), may hold values from 1 to 976, as said below
- w_qkv: bfloat16 [2, 1024, 3, 1024], P(None, 'dp', None, 'tensor'), may hold values from -0.1875 to 0.1875
- b_qv: bfloat16 [2, 2, 1024], replicated, may hold values from -3 to 3
- w_out: bfloat16 [2, 1024, 1024], P(None, 'tensor', 'dp'), may hold values from -0.5 to 0.5
- b_out: bfloat16 [2, 1024], replicated, may hold values from -3 to 3
- w_in: bfloat16 [2, 1024, 4096], P(None, 'dp', 'tensor'), may hold values from -0.1875 to 0.1875
- b_in: bfloat16 [2, 4096], replicated, may hold values from -3 to 3
- w_down: bfloat16 [2, 4096, 1024], P(None, 'tensor', 'dp'), may hold values from -0.09375 to 0.09375
- b_down: bfloat16 [2, 1024], replicated, may hold values from -3 to 3
- ln_gain: bfloat16 [2, 2, 1024], replicated, may hold values from 0.5 to 1.5
- ln_bias: bfloat16 [2, 2, 1024], replicated, may hold values from -2 to 2
- cotangent: bfloat16 [16384, 1024], P(('dp', 'tensor')), may hold values from -6 to 6
Outputs:
- encoded: bfloat16 [16384, 1024], P(('dp', 'tensor'))
- g_tokens: bfloat16 [16384, 1024], P(('dp', 'tensor'))
- g_w_qkv: float32 [2, 1024, 3, 1024], P(None, 'dp', None, 'tensor')
- g_b_qv: float32 [2, 2, 1024], replicated
- g_w_out: float32 [2, 1024, 1024], P(None, 'tensor', 'dp')
- g_b_out: float32 [2, 1024], replicated
- g_w_in: float32 [2, 1024, 4096], P(None, 'dp', 'tensor')
- g_b_in: float32 [2, 4096], replicated
- g_w_down: float32 [2, 4096, 1024], P(None, 'tensor', 'dp')
- g_b_down: float32 [2, 1024], replicated
- g_ln_gain: float32 [2, 2, 1024], replicated
- g_ln_bias: float32 [2, 2, 1024], replicated
Inputs may be any that keep to these rules, and one draw needn't show every extreme that they name: In each data shard exactly one sequence, at a place drawn from the seed, is long: between 897 and 976 tokens, with exactly 976 in some shard; the others have at most 16 tokens each. A shard's lengths sum to at most 1024.
All inputs are finite; a program needn't handle non-finite values.
Results may differ from a plain program's by a relative error of at most 0.028.
Values may be sent and summed in bfloat16 or wider, within the bound.
A program may use at most 128 MiB of HBM per device.

v0:
```python
import functools

import jax
import jax.numpy as jnp
from jax import lax
from jax.experimental import pallas as pl
from jax.experimental.pallas import tpu as pltpu
from jax.sharding import PartitionSpec as P

DH = 64
EPSILON = 1e-06
MESH = pl.DeviceIdType.MESH
F32 = jnp.float32
BF16 = jnp.bfloat16


def place():
    dp, tensor = lax.axis_index("dp"), lax.axis_index("tensor")
    core = lax.rem(dp, 2)
    z = lax.rem(lax.div(dp, 2), 4)
    x = lax.rem(lax.div(tensor, 4) * 2 + lax.div(dp, 8), 4)
    y = lax.rem(tensor, 4)
    return x, y, z, core


def device(x, y, z, core):
    x, y, z = lax.rem(x, 4), lax.rem(y, 4), lax.rem(z, 4)
    return (lax.rem(x, 2) * 8 + z * 2 + core, lax.div(x, 2) * 4 + y)


def block_of(x, z):
    x, z = lax.rem(x, 4), lax.rem(z, 4)
    return lax.rem(x, 2) * 8 + z * 2 + lax.div(x, 2)


def greet(devices):
    barrier = pltpu.get_barrier_semaphore()
    for other in devices:
        pl.semaphore_signal(barrier, inc=1, device_id=other, device_id_type=MESH)
    pl.semaphore_wait(barrier, len(devices))


class Copies:
    def __init__(self, send, recv):
        self.send, self.recv, self.started = send, recv, []

    def start(self, src, dst, to):
        at = len(self.started)
        copy = pltpu.make_async_remote_copy(
            src_ref=src,
            dst_ref=dst,
            send_sem=self.send.at[at],
            recv_sem=self.recv.at[at],
            device_id=to,
            device_id_type=MESH,
        )
        copy.start()
        self.started.append(copy)
        return copy

    def wait_sends(self):
        for copy in self.started:
            copy.wait_send()


def group_neighbours():
    x, y, z, core = place()
    return (
        device(x, y, z, 1 - core),
        device(x, y + 1, z, core),
        device(x, y + 3, z, core),
    )


GATHER_COPIES = 24
SCATTER_COPIES = 20


def gather_steps(copies, out, base, count):
    x, y, z, core = place()
    pair, after, before = group_neighbours()
    half = count // 2
    top, low, both = pl.ds(base, half), pl.ds(base + half, half), pl.ds(base, count)

    def send(step, rows, to):
        ref = out.at[core * 4 + lax.rem(y + step, 4), rows]
        return copies.start(ref, ref, to)

    top_after = send(0, top, after)
    low_before = send(0, low, before)
    low_after = send(0, low, after)
    top_before = send(0, top, before)
    own_pair = send(0, both, pair)
    yield
    top_after.wait_recv()
    far_top = send(3, top, after)
    low_before.wait_recv()
    far_low = send(1, low, before)
    yield
    low_after.wait_recv()
    pair_before = send(3, both, pair)
    top_before.wait_recv()
    pair_after = send(1, both, pair)
    yield
    far_top.wait_recv()
    pair_top = send(2, top, pair)
    far_low.wait_recv()
    pair_low = send(2, low, pair)
    yield
    for copy in (own_pair, pair_before, pair_after, pair_top, pair_low):
        copy.wait_recv()
    yield


def scatter_steps(copies, part, from_pair, staged, far, near, base, count, result):
    x, y, z, core = place()
    pair, after, before = group_neighbours()
    half = count // 2
    top, low, both = pl.ds(base, half), pl.ds(base + half, half), pl.ds(base, count)
    here, there = core * 4, (1 - core) * 4
    steps = (2, 1, 3, 0)
    swaps = [
        copies.start(
            part.at[there + lax.rem(y + step, 4), both], from_pair.at[slot, both], pair
        )
        for slot, step in enumerate(steps)
    ]

    def chip(slot, rows):
        own = part[here + lax.rem(y + steps[slot], 4), rows].astype(F32)
        return own + from_pair[slot, rows].astype(F32)

    yield
    swaps[0].wait_recv()
    staged[0, top] = chip(0, top).astype(BF16)
    far_top = copies.start(staged.at[0, top], far.at[top], after)
    staged[0, low] = chip(0, low).astype(BF16)
    far_low = copies.start(staged.at[0, low], far.at[low], before)
    yield
    swaps[1].wait_recv()
    staged[1, low] = chip(1, low).astype(BF16)
    low_after = copies.start(staged.at[1, low], near.at[0, low], after)
    swaps[2].wait_recv()
    staged[2, top] = chip(2, top).astype(BF16)
    top_before = copies.start(staged.at[2, top], near.at[1, top], before)
    yield
    far_top.wait_recv()
    staged[1, top] = (chip(1, top) + far[top].astype(F32)).astype(BF16)
    top_after = copies.start(staged.at[1, top], near.at[0, top], after)
    far_low.wait_recv()
    staged[2, low] = (chip(2, low) + far[low].astype(F32)).astype(BF16)
    low_before = copies.start(staged.at[2, low], near.at[1, low], before)
    yield
    swaps[3].wait_recv()
    own = chip(3, both)
    for copy in (low_after, top_before, top_after, low_before):
        copy.wait_recv()
    result.append(own + near[0, both].astype(F32) + near[1, both].astype(F32))
    yield


def scatter_gather(scatter, gather, part, bufs, rows_out, between, tick):
    x, y, z, core = place()
    count = part.shape[1] // 2
    results = [], []
    first, second = [
        scatter_steps(scatter, part, *bufs, at * count, count, results[at]) for at in (0, 1)
    ]

    def send(at):
        rows = pl.ds(at * count, count)
        rows_out[core * 4 + y, rows] = between(results[at][0], at, rows)
        steps = gather_steps(gather, rows_out, at * count, count)
        next(steps)
        return steps

    next(first)
    next(second)
    tick()
    next(first)
    next(first)
    next(second)
    next(first)
    next(second)
    tick()
    next(second)
    next(first)
    first = send(0)
    tick()
    next(second)
    second = send(1)
    next(first)
    tick()
    next(first)
    next(second)
    next(first)
    tick()
    next(second)
    next(first)
    next(second)
    tick()
    next(second)


def gather_all(gather, rows_out, tick):
    count = rows_out.shape[1] // 2
    first, second = [gather_steps(gather, rows_out, at * count, count) for at in (0, 1)]
    for _ in range(5):
        next(first)
        next(second)
        tick()


def scatter_all(scatter, part, bufs, tick):
    count = part.shape[1] // 2
    results = [], []
    first, second = [
        scatter_steps(scatter, part, *bufs, at * count, count, results[at]) for at in (0, 1)
    ]
    for _ in range(5):
        next(first)
        next(second)
        tick()
    return results[0][0], results[1][0]


def scatter_scratch(rows, width):
    return [
        pltpu.VMEM((4, rows, width), BF16),
        pltpu.VMEM((3, rows, width), BF16),
        pltpu.VMEM((rows, width), BF16),
        pltpu.VMEM((2, rows, width), BF16),
    ]


def sems(count):
    return [pltpu.SemaphoreType.DMA((count,)), pltpu.SemaphoreType.DMA((count,))]


def plane_ring(axis):
    x, y, z, core = place()
    if axis == "x":
        return device(x + 1, y, z, core), device(x + 3, y, z, core)
    return device(x, y, z + 1, core), device(x, y, z + 3, core)


def plane_at(first, u, v):
    return block_of(u, v) if first == "x" else block_of(v, u)


PLANE_GATHER_COPIES = 36
PLANE_SCATTER_COPIES = 36


def gather_plane(copies, out):
    x, y, z, core = place()
    quarter = out.shape[1] // 4
    paths = []
    for first, base in (("x", 0), ("z", 2 * quarter)):
        v, u = (x, z) if first == "x" else (z, x)
        other = "z" if first == "x" else "x"
        paths.append(
            dict(
                first=first,
                v=v,
                u=u,
                ring=plane_ring(first),
                cross=plane_ring(other),
                halves=(pl.ds(base, quarter), pl.ds(base + quarter, quarter)),
                whole=pl.ds(base, 2 * quarter),
            )
        )

    def send(path, dv, du, rows, to):
        at = plane_at(path["first"], path["v"] + dv, path["u"] + du)
        return copies.start(out.at[at, rows], out.at[at, rows], to)

    for path in paths:
        after, before = path["ring"]
        top, low = path["halves"]
        path["ta"] = send(path, 0, 0, top, after)
        path["lb"] = send(path, 0, 0, low, before)
        path["la"] = send(path, 0, 0, low, after)
        path["tb"] = send(path, 0, 0, top, before)
        path["c"] = {0: [send(path, 0, 0, path["whole"], to) for to in path["cross"]]}
    yield
    for path in paths:
        path["ta"].wait_recv()
        path["ft"] = send(path, 3, 0, path["halves"][0], path["ring"][0])
        path["lb"].wait_recv()
        path["fl"] = send(path, 1, 0, path["halves"][1], path["ring"][1])
    yield
    for path in paths:
        path["la"].wait_recv()
        path["c"][3] = [send(path, 3, 0, path["whole"], to) for to in path["cross"]]
        path["tb"].wait_recv()
        path["c"][1] = [send(path, 1, 0, path["whole"], to) for to in path["cross"]]
    last = []
    for path in paths:
        path["c"][0][0].wait_recv()
        last.append(send(path, 0, 3, path["whole"], path["cross"][0]))
    yield
    for path in paths:
        path["ft"].wait_recv()
        path["fl"].wait_recv()
        path["c"][2] = [send(path, 2, 0, path["whole"], to) for to in path["cross"]]
    yield
    for path in paths:
        path["c"][3][0].wait_recv()
        last.append(send(path, 3, 3, path["whole"], path["cross"][0]))
        path["c"][1][1].wait_recv()
        last.append(send(path, 1, 1, path["whole"], path["cross"][1]))
    yield
    for path in paths:
        path["c"][2][1].wait_recv()
        last.append(send(path, 2, 1, path["whole"], path["cross"][1]))
    yield
    for path in paths:
        for copy in (path["c"][0][1], path["c"][3][1], path["c"][1][0], path["c"][2][0]):
            copy.wait_recv()
    for copy in last:
        copy.wait_recv()


def scatter_plane_scratch(rows, width):
    half = rows // 2
    return [
        pltpu.VMEM((2, 4, half, width), BF16),
        pltpu.VMEM((2, 2, 4, half, width), BF16),
        pltpu.VMEM((2, 4, half, width), BF16),
        pltpu.VMEM((2, 4, half, width), BF16),
        pltpu.VMEM((2, half, width), BF16),
        pltpu.VMEM((2, 2, half, width), BF16),
        pltpu.VMEM((2, 2, half // 2, width), BF16),
    ]


def scatter_plane(copies, part, out, far, near, passed, summed, far2, near2, passed2):
    x, y, z, core = place()
    half = part.shape[1] // 2
    quarter = half // 2
    paths = []
    for at, (first, base) in enumerate((("x", 0), ("z", half))):
        u, v = (x, z) if first == "x" else (z, x)
        other = "z" if first == "x" else "x"
        paths.append(
            dict(
                at=at,
                first=first,
                u=u,
                v=v,
                ring=plane_ring(first),
                cross=plane_ring(other),
                rows=pl.ds(base, half),
                base=base,
            )
        )

    def source(path, du, v):
        return (plane_at(path["first"], path["u"] + du, v), path["rows"])

    for path in paths:
        at, (after, before) = path["at"], path["ring"]
        path["far"] = [
            copies.start(
                part.at[source(path, 2, v)], far.at[at, v], after if v < 2 else before
            )
            for v in range(4)
        ]
    for path in paths:
        at, (after, before) = path["at"], path["ring"]
        path["near"] = [
            copies.start(part.at[source(path, 1, v)], near.at[at, 0, v], after) for v in (2, 3)
        ] + [
            copies.start(part.at[source(path, 3, v)], near.at[at, 1, v], before) for v in (0, 1)
        ]
    yield
    for path in paths:
        at, (after, before) = path["at"], path["ring"]
        for v in (0, 2, 1, 3):
            path["far"][v].wait_recv()
            du, slot, to = (1, 0, after) if v < 2 else (3, 1, before)
            own = part[source(path, du, v)].astype(F32)
            passed[at, v] = (own + far[at, v].astype(F32)).astype(BF16)
            path["near"].append(copies.start(passed.at[at, v], near.at[at, slot, v], to))
    yield
    for path in paths:
        at = path["at"]
        for copy in path["near"]:
            copy.wait_recv()
        for v in range(4):
            own = part[source(path, 0, v)].astype(F32)
            summed[at, v] = (
                own + near[at, 0, v].astype(F32) + near[at, 1, v].astype(F32)
            ).astype(BF16)
        v, (after, before) = path["v"], path["cross"]
        top, low = pl.ds(0, quarter), pl.ds(quarter, quarter)
        v1, v2, v3 = lax.rem(v + 1, 4), lax.rem(v + 2, 4), lax.rem(v + 3, 4)
        path["ft"] = copies.start(summed.at[at, v2, top], far2.at[at, top], after)
        path["fl"] = copies.start(summed.at[at, v2, low], far2.at[at, low], before)
        path["last"] = [
            copies.start(summed.at[at, v1, low], near2.at[at, 0, low], after),
            copies.start(summed.at[at, v3, top], near2.at[at, 1, top], before),
        ]
    yield
    for path in paths:
        at, v, (after, before) = path["at"], path["v"], path["cross"]
        top, low = pl.ds(0, quarter), pl.ds(quarter, quarter)
        v1, v3 = lax.rem(v + 1, 4), lax.rem(v + 3, 4)
        path["ft"].wait_recv()
        passed2[at, 0] = (summed[at, v1, top].astype(F32) + far2[at, top].astype(F32)).astype(BF16)
        path["last"].append(copies.start(passed2.at[at, 0], near2.at[at, 0, top], after))
        path["fl"].wait_recv()
        passed2[at, 1] = (summed[at, v3, low].astype(F32) + far2[at, low].astype(F32)).astype(BF16)
        path["last"].append(copies.start(passed2.at[at, 1], near2.at[at, 1, low], before))
    yield
    for path in paths:
        at, v = path["at"], path["v"]
        for copy in path["last"]:
            copy.wait_recv()
        total = summed[at, v].astype(F32) + near2[at, 0].astype(F32) + near2[at, 1].astype(F32)
        out[path["rows"]] = total.astype(out.dtype)


def params(number):
    return pltpu.CompilerParams(
        collective_id=number, has_side_effects=True, vmem_limit_bytes=48 * 2**20
    )


VMEM = pl.BlockSpec(memory_space=pltpu.VMEM)


def neighbours():
    return [*group_neighbours(), *plane_ring("x"), *plane_ring("z")]


def drain(steps):
    for _ in steps:
        pass


def swap_partner():
    x, y, z, core = place()
    upper = lax.div(x, 2)
    return core != upper, device(core * 2 + lax.rem(x, 2), y, z, upper)


def greet_with_partner(others):
    moves, partner = swap_partner()
    barrier = pltpu.get_barrier_semaphore()
    for other in others:
        pl.semaphore_signal(barrier, inc=1, device_id=other, device_id_type=MESH)

    @pl.when(moves)
    def _():
        pl.semaphore_signal(barrier, inc=1, device_id=partner, device_id_type=MESH)

    pl.semaphore_wait(barrier, len(others) + moves.astype(jnp.int32))


def partner_copy(src, dst, send, recv):
    return pltpu.make_async_remote_copy(
        src_ref=src,
        dst_ref=dst,
        send_sem=send,
        recv_sem=recv,
        device_id=swap_partner()[1],
        device_id_type=MESH,
    )


class Swaps:
    def __init__(self, send, recv):
        self.send, self.recv, self.moves = send, recv, []

    def copy(self, src, dst, own_dst=None):
        at = len(self.moves)
        copy = partner_copy(src, dst, self.send.at[at], self.recv.at[at])
        self.moves.append(copy)
        moves, _ = swap_partner()

        @pl.when(moves)
        def _():
            copy.start()

        @pl.when(jnp.logical_not(moves))
        def _():
            target = dst if own_dst is None else own_dst
            target[...] = src[...]

        return copy

    def arrive(self, copy):
        @pl.when(swap_partner()[0])
        def _():
            copy.wait_recv()

    def finish(self, *arrived):
        @pl.when(swap_partner()[0])
        def _():
            for copy in self.moves:
                copy.wait_send()
                if not any(copy is other for other in arrived):
                    copy.wait_recv()


def start_kernel(
    tokens, weights, lengths, later, rows_out, weights_out, lengths_out, later_out,
    ssend, srecv, send, recv, wsend, wrecv,
):
    x, y, z, core = place()
    greet_with_partner(neighbours())
    plane, group, swaps = Copies(wsend, wrecv), Copies(send, recv), Swaps(ssend, srecv)
    there = block_of(core * 2 + lax.rem(x, 2), z)
    own = weights_out.at[block_of(x, z)]
    weights_move = swaps.copy(weights, weights_out.at[there], own)
    own = rows_out.at[core * 4 + y]
    rows_move = swaps.copy(tokens, rows_out.at[lax.div(x, 2) * 4 + y], own)
    swaps.copy(lengths, lengths_out)
    swaps.copy(later, later_out)
    swaps.arrive(weights_move)
    steps = gather_plane(plane, weights_out)
    next(steps)
    swaps.arrive(rows_move)
    gather_all(group, rows_out, lambda: next(steps, None))
    drain(steps)
    swaps.finish(weights_move, rows_move)
    group.wait_sends()
    plane.wait_sends()


def start(tokens, weights, lengths, later):
    rows, width = tokens.shape
    held, columns = weights.shape
    gathered, full, lengths, later = pl.pallas_call(
        start_kernel,
        out_shape=(
            jax.ShapeDtypeStruct((8, rows, width), BF16),
            jax.ShapeDtypeStruct((16, held, columns), BF16),
            jax.ShapeDtypeStruct(lengths.shape, lengths.dtype),
            jax.ShapeDtypeStruct(later.shape, BF16),
        ),
        in_specs=[VMEM] * 4,
        out_specs=(VMEM,) * 4,
        scratch_shapes=sems(4) + sems(GATHER_COPIES) + sems(PLANE_GATHER_COPIES),
        compiler_params=params(0),
        name="start",
    )(tokens, weights, lengths, later)
    return gathered.reshape(8 * rows, width), full.reshape(16 * held, columns), lengths, later


def normed_parts(stream):
    row_mean = jnp.mean(stream, axis=-1, keepdims=True)
    centered = stream - row_mean
    row_var = jnp.mean(centered * centered, axis=-1, keepdims=True)
    scale = lax.rsqrt(row_var + EPSILON)
    return centered * scale, scale


def norm_pull(unit, scale, gain, grad, sums):
    scaled = grad * gain
    inner = jnp.mean(scaled * unit, axis=-1, keepdims=True)
    pulled = scale * (scaled - jnp.mean(scaled, axis=-1, keepdims=True) - unit * inner)
    low = pulled.astype(BF16)
    sums[0:1] += jnp.sum(grad * unit, axis=0, keepdims=True)
    sums[1:2] += jnp.sum(grad, axis=0, keepdims=True)
    sums[2:3] += jnp.sum(low.astype(F32), axis=0, keepdims=True)
    return pulled, low


def group_kernel(mode, plane_mode, swapped, count, kept, refs):
    refs = list(refs)
    take = lambda number: [refs.pop(0) for _ in range(number)]
    part, held, vectors, *extra = take(count)
    plane_in = take(1)[0] if plane_mode else None
    swaps_in = take(swapped)
    outs = take(kept)
    (rows_out,) = take(1)
    plane_out = take(1)[0] if plane_mode else None
    swaps_out = take(swapped)
    bufs = take(4)
    scatter, gather = Copies(*take(2)), Copies(*take(2))
    x, y, z, core = place()
    others = neighbours() if plane_mode else group_neighbours()
    if swapped:
        swaps = Swaps(*take(2))
        greet_with_partner(others)
    else:
        greet(others)
    steps = iter(())
    if plane_mode == "gather":
        plane = Copies(*take(2))
        plane_out[block_of(x, z)] = plane_in[...]
        steps = gather_plane(plane, plane_out)
    elif plane_mode == "scatter":
        plane = Copies(*take(2))
        steps = scatter_plane(plane, plane_in, plane_out, *refs)

    def tick():
        next(steps, None)

    gain, shift = vectors[1:2], vectors[2:3]
    if mode != "forward":
        sums = outs[-1]
        sums[...] = jnp.zeros_like(sums)

    def between(total, at, rows):
        if mode == "forward":
            stream = held[rows] + total + vectors[0:1]
            outs[0][rows] = stream
            unit, _ = normed_parts(stream)
            normed = unit * gain + shift
            outs[1][rows] = normed
            return normed.astype(BF16)
        if mode == "turn":
            unit, scale = normed_parts(held[rows] + total + vectors[0:1])
            outs[0][rows] = (unit * gain + shift).astype(BF16)
            pulled, low = norm_pull(unit, scale, gain, extra[0][rows].astype(F32), sums)
            outs[1][rows] = pulled
            return low
        unit, scale = normed_parts(extra[0][rows])
        pulled, low = norm_pull(unit, scale, gain, held[rows] + total, sums)
        outs[0][rows] = pulled
        return low

    def first_tick():
        if not started:
            started.append(True)
            for src, dst in zip(swaps_in, swaps_out):
                swaps.copy(src, dst)
        tick()

    started = []
    scatter_gather(scatter, gather, part, bufs, rows_out, between, first_tick)
    drain(steps)
    scatter.wait_sends()
    gather.wait_sends()
    if plane_mode:
        plane.wait_sends()
    if swapped:
        swaps.finish()


def group_call(mode, number, operands, outs, plane_mode=None, plane_in=None, swapped=()):
    part = operands[0]
    rows, width = part.shape[0] // 8, part.shape[1]
    shapes = tuple(jax.ShapeDtypeStruct(shape, kind) for shape, kind in outs)
    shapes += (jax.ShapeDtypeStruct((8, rows, width), BF16),)
    scratch = scatter_scratch(rows, width) + sems(SCATTER_COPIES) + sems(GATHER_COPIES)
    given = [part.reshape(8, rows, width), *operands[1:]]
    if swapped:
        scratch += sems(len(swapped))
    if plane_mode == "gather":
        kept, columns = plane_in.shape
        shapes += (jax.ShapeDtypeStruct((16, kept, columns), BF16),)
        scratch += sems(PLANE_GATHER_COPIES)
        given.append(plane_in)
    elif plane_mode == "scatter":
        kept, columns = plane_in.shape[0] // 16, plane_in.shape[1]
        shapes += (jax.ShapeDtypeStruct((kept, columns), BF16),)
        scratch += sems(PLANE_SCATTER_COPIES) + scatter_plane_scratch(kept, columns)
        given.append(plane_in.reshape(16, kept, columns))
    shapes += tuple(jax.ShapeDtypeStruct(array.shape, array.dtype) for array in swapped)
    given += swapped

    def kernel(*refs):
        group_kernel(mode, plane_mode, len(swapped), len(operands), len(outs), refs)

    results = pl.pallas_call(
        kernel,
        out_shape=shapes,
        in_specs=[VMEM] * len(given),
        out_specs=(VMEM,) * len(shapes),
        scratch_shapes=scratch,
        compiler_params=params(number),
        name=mode + str(number),
    )(*given)
    results = list(results)
    at = len(outs)
    results[at] = results[at].reshape(8 * rows, width)
    if plane_mode == "gather":
        results[at + 1] = results[at + 1].reshape(16 * kept, columns)
    return results


def sum_small(copies, small, out, got_x, got_z):
    x, y, z, core = place()
    own = core * 4 + y
    along_x = [device(x + step, y, z, core) for step in (1, 2, 3)]
    along_z = [device(x, y, z + step, core) for step in (1, 2, 3)]
    along_y = [device(x, y + step, z, core) for step in (1, 2, 3)]
    first = [copies.start(small, got_x.at[at], to) for at, to in enumerate(along_x)]
    yield
    for copy in first:
        copy.wait_recv()
    got_z[3] = small[...] + got_x[0] + got_x[1] + got_x[2]
    second = [copies.start(got_z.at[3], got_z.at[at], to) for at, to in enumerate(along_z)]
    yield
    for copy in second:
        copy.wait_recv()
    out[own] = got_z[3] + got_z[0] + got_z[1] + got_z[2]
    third = [copies.start(out.at[own], out.at[own], to) for to in along_y]
    yield
    for copy in third:
        copy.wait_recv()
    held = out.at[pl.ds(core * 4, 4)]
    copies.start(held, held, device(x, y, z, 1 - core)).wait_recv()


def end_kernel(
    part, held, grads, small, later, rows_out, grads_out, small_out, later_out,
    from_pair, staged, far, near, pfar, pnear, passed, summed, far2, near2, passed2,
    rows_stage, grads_stage, got_x, got_z,
    ssend, srecv, send, recv, psend, precv, tsend, trecv,
):
    x, y, z, core = place()
    greet_with_partner(
        neighbours()
        + [device(x + 2, y, z, core), device(x, y + 2, z, core), device(x, y, z + 2, core)]
    )
    group, plane, tiny = Copies(send, recv), Copies(psend, precv), Copies(tsend, trecv)
    swaps = Swaps(ssend, srecv)
    tiny_steps = sum_small(tiny, small, small_out, got_x, got_z)
    plane_steps = scatter_plane(
        plane, grads, grads_stage, pfar, pnear, passed, summed, far2, near2, passed2
    )
    started = []

    def tick():
        next(plane_steps, None)
        next(tiny_steps, None)
        if not started:
            started.append(swaps.copy(later, later_out))

    totals = scatter_all(group, part, (from_pair, staged, far, near), tick)
    count = rows_stage.shape[0] // 2
    for at in (0, 1):
        rows = pl.ds(at * count, count)
        rows_stage[rows] = (held[rows] + totals[at]).astype(BF16)
    swaps.copy(rows_stage, rows_out)
    drain(plane_steps)
    swaps.copy(grads_stage, grads_out)
    drain(tiny_steps)
    swaps.finish()
    group.wait_sends()
    plane.wait_sends()
    tiny.wait_sends()


def end(part, held, grads, small, later):
    rows, width = held.shape
    kept, columns = grads.shape[0] // 16, grads.shape[1]
    return pl.pallas_call(
        end_kernel,
        out_shape=(
            jax.ShapeDtypeStruct((rows, width), BF16),
            jax.ShapeDtypeStruct((kept, columns), BF16),
            jax.ShapeDtypeStruct((8, *small.shape), F32),
            jax.ShapeDtypeStruct(later.shape, BF16),
        ),
        in_specs=[VMEM] * 5,
        out_specs=(VMEM,) * 4,
        scratch_shapes=scatter_scratch(rows, width)
        + scatter_plane_scratch(kept, columns)
        + [
            pltpu.VMEM((rows, width), BF16),
            pltpu.VMEM((kept, columns), BF16),
            pltpu.VMEM((3, *small.shape), F32),
            pltpu.VMEM((4, *small.shape), F32),
        ]
        + sems(3)
        + sems(SCATTER_COPIES)
        + sems(PLANE_SCATTER_COPIES)
        + sems(10),
        compiler_params=params(1),
        name="end",
    )(part.reshape(8, rows, width), held, grads.reshape(16, kept, columns), small, later)


def segment_ids(shard_lengths, total_rows, seq_count):
    seq_ends = jnp.cumsum(shard_lengths)
    positions = jnp.arange(total_rows, dtype=jnp.int32)
    segments = jnp.sum((positions[:, None] >= seq_ends[None, :]).astype(jnp.int32), axis=1)
    return jnp.where(segments == seq_count, seq_count + positions, segments)


def masked_scores(queries, keys_in, allowed, score_scale):
    scores = (
        jnp.einsum("qhd,khd->hqk", queries, keys_in, preferred_element_type=jnp.float32)
        * score_scale
    )
    return jnp.where(allowed[None], scores, -1e30)


def attend_forward(queries, keys_in, values_in, allowed, score_scale):
    scores = masked_scores(queries, keys_in, allowed, score_scale)
    row_peak = jnp.max(scores, axis=-1, keepdims=True)
    exp_scores = jnp.exp(scores - row_peak)
    row_total = jnp.sum(exp_scores, axis=-1, keepdims=True)
    attn_probs = (exp_scores / row_total).astype(jnp.bfloat16)
    context = jnp.einsum("hqk,khd->qhd", attn_probs, values_in, preferred_element_type=jnp.float32)
    return (context, row_peak + jnp.log(row_total))


def attend_backward(queries, keys_in, values_in, allowed, score_scale, log_total, grad_context):
    scores = masked_scores(queries, keys_in, allowed, score_scale)
    attn_probs = jnp.exp(scores - log_total)
    probs_low = attn_probs.astype(jnp.bfloat16)
    grad_probs = jnp.einsum(
        "qhd,khd->hqk", grad_context, values_in, preferred_element_type=jnp.float32
    )
    grad_values = jnp.einsum(
        "hqk,qhd->khd", probs_low, grad_context, preferred_element_type=jnp.float32
    )
    row_inner = jnp.sum(attn_probs * grad_probs, axis=-1, keepdims=True)
    grad_scores = (attn_probs * (grad_probs - row_inner)).astype(jnp.bfloat16)
    grad_queries = (
        jnp.einsum("hqk,khd->qhd", grad_scores, keys_in, preferred_element_type=jnp.float32)
        * score_scale
    )
    grad_keys = (
        jnp.einsum("hqk,qhd->khd", grad_scores, queries, preferred_element_type=jnp.float32)
        * score_scale
    )
    return (grad_queries, grad_keys, grad_values)


def exact_gelu(values):
    return jax.nn.gelu(values, approximate=False)


CONTRACT_LAST = (((1,), (1,)), ((), ()))
CONTRACT_FIRST = (((0,), (0,)), ((), ()))


def shards(
    tokens,
    lengths,
    w_qkv,
    b_qv,
    w_out,
    b_out,
    w_in,
    b_in,
    w_down,
    b_down,
    ln_gain,
    ln_bias,
    cotangent,
):
    x, y, z, core = place()
    column = core * 4 + y
    own_rows, width = tokens.shape
    total_rows = own_rows * 8
    layers, kept = w_qkv.shape[:2]
    col_width = w_qkv.shape[3]
    hidden_width = w_in.shape[2]
    head_count = col_width // DH
    score_scale = DH ** (-0.5)
    cuts = (0, 3 * col_width, 4 * col_width, 4 * col_width + hidden_width)

    cut_out, cut_down = 3 * col_width, hidden_width
    attention_shards = [
        jnp.concatenate([w_qkv[at].reshape(kept, 3 * col_width), w_out[at].T], axis=1)
        for at in range(layers)
    ]
    hidden_shards = [
        jnp.concatenate([w_in[at], w_down[at].T], axis=1) for at in range(layers)
    ]
    later_shard = jnp.concatenate([attention_shards[1], hidden_shards[1]], axis=1)
    seq_count = lengths.shape[1]
    lengths = jnp.pad(lengths, ((0, 7), (0, 128 - seq_count)))
    attn_input, attention_full, lengths, first_hidden = start(
        tokens, attention_shards[0], lengths, hidden_shards[0]
    )
    hidden = lax.dynamic_slice_in_dim(attn_input, column * own_rows, own_rows, 0).astype(F32)

    segments = segment_ids(lengths[0, :seq_count], total_rows, seq_count)
    allowed = segments[:, None] == segments[None, :]

    def vectors(bias, at, which):
        rows = [bias.astype(F32), ln_gain[at, which].astype(F32), ln_bias[at, which].astype(F32)]
        return jnp.stack(rows + [jnp.zeros_like(rows[0])] * 5)

    row_kind = ((own_rows, width), F32)
    sum_kind = ((8, width), F32)
    low_kind = ((own_rows, width), BF16)
    stored = []
    for at in range(layers):
        if at > 0:
            attention_full, hidden_full = (
                later_full[:, : cut_out + col_width],
                later_full[:, cut_out + col_width :],
            )
        full_qkv, full_out = attention_full[:, :cut_out], attention_full[:, cut_out:]
        bias_qv = lax.dynamic_slice_in_dim(
            b_qv[at].astype(F32), column * col_width, col_width, 1
        )
        bias_all = jnp.concatenate([bias_qv[0], jnp.zeros_like(bias_qv[0]), bias_qv[1]])
        qkv = jnp.dot(attn_input, full_qkv, preferred_element_type=F32)
        qkv_low = (qkv + bias_all).astype(BF16)
        head_view = qkv_low.reshape(total_rows, 3, head_count, DH)
        context, log_total = attend_forward(
            head_view[:, 0], head_view[:, 1], head_view[:, 2], allowed, score_scale
        )
        context_low = context.reshape(total_rows, col_width).astype(BF16)
        branch = lax.dot_general(
            context_low, full_out, CONTRACT_LAST, preferred_element_type=F32
        ).astype(BF16)
        first_vectors = vectors(b_out[at], at, 0)
        if at == 0:
            first_sum, normed, mlp_input, hidden_full, later_shard, cotangent = group_call(
                "forward", 2, (branch, hidden, first_vectors), (row_kind, row_kind),
                "gather", first_hidden, (later_shard, cotangent),
            )
        else:
            first_sum, normed, mlp_input = group_call(
                "forward", 3, (branch, hidden, first_vectors), (row_kind, row_kind)
            )
        full_in, full_down = hidden_full[:, :cut_down], hidden_full[:, cut_down:]
        bias_in = lax.dynamic_slice_in_dim(
            b_in[at].astype(F32), column * hidden_width, hidden_width, 0
        )
        pre_gelu = jnp.dot(mlp_input, full_in, preferred_element_type=F32) + bias_in
        act_low = exact_gelu(pre_gelu).astype(BF16)
        branch = lax.dot_general(
            act_low, full_down, CONTRACT_LAST, preferred_element_type=F32
        ).astype(BF16)
        second_vectors = vectors(b_down[at], at, 1)
        stored.append(
            [attn_input, qkv_low, log_total, context_low, first_sum, mlp_input, pre_gelu,
             act_low, first_vectors, second_vectors, full_qkv, full_out, full_in, full_down]
        )
        if at == 0:
            second_sum, hidden, attn_input, later_full = group_call(
                "forward", 4, (branch, normed, second_vectors), (row_kind, row_kind),
                "gather", later_shard,
            )
            stored[at].append(second_sum)
        else:
            encoded, grad_second, sums_two, down_full = group_call(
                "turn",
                5,
                (branch, normed, second_vectors, cotangent),
                (low_kind, row_kind, sum_kind),
            )

    attention_grads, hidden_grads = [None] * layers, [None] * layers
    small_list = [None] * layers
    for at in reversed(range(layers)):
        (
            attn_input, qkv_low, log_total, context_low, first_sum, mlp_input, pre_gelu,
            act_low, first_vectors, second_vectors, full_qkv, full_out, full_in, full_down,
        ) = stored[at][:14]
        grad_act = jnp.dot(down_full, full_down, preferred_element_type=F32)
        grad_w_down = lax.dot_general(
            down_full, act_low, CONTRACT_FIRST, preferred_element_type=F32
        )
        pre_low = jax.vjp(exact_gelu, pre_gelu)[1](grad_act)[0].astype(BF16)
        grad_w_in = lax.dot_general(
            mlp_input, pre_low, CONTRACT_FIRST, preferred_element_type=F32
        )
        branch = lax.dot_general(
            pre_low, full_in, CONTRACT_LAST, preferred_element_type=F32
        ).astype(BF16)
        own_grads = jnp.concatenate([grad_w_in.astype(BF16), grad_w_down.astype(BF16)], axis=1)
        held_back = (encoded,) if at > 0 else (attention_grads[1],)
        grad_first, sums_one, attn_full, hidden_grads[at], *swapped = group_call(
            "backward", 6 + 2 * at, (branch, grad_second, first_vectors, first_sum),
            (row_kind, sum_kind), "scatter", own_grads, held_back,
        )
        if at > 0:
            (encoded,) = swapped
        else:
            (attention_grads[1],) = swapped
        grad_context = jnp.dot(attn_full, full_out, preferred_element_type=F32)
        grad_context_low = grad_context.astype(BF16).reshape(total_rows, head_count, DH)
        grad_w_out = lax.dot_general(
            attn_full, context_low, CONTRACT_FIRST, preferred_element_type=F32
        )
        head_view = qkv_low.reshape(total_rows, 3, head_count, DH)
        grad_queries, grad_keys, grad_values = attend_backward(
            head_view[:, 0], head_view[:, 1], head_view[:, 2],
            allowed, score_scale, log_total, grad_context_low,
        )
        grad_qkv_low = (
            jnp.stack([grad_queries, grad_keys, grad_values], axis=1)
            .reshape(total_rows, 3 * col_width)
            .astype(BF16)
        )
        grad_w_qkv = lax.dot_general(
            attn_input, grad_qkv_low, CONTRACT_FIRST, preferred_element_type=F32
        )
        branch = lax.dot_general(
            grad_qkv_low, full_qkv, CONTRACT_LAST, preferred_element_type=F32
        ).astype(BF16)
        own_grads = jnp.concatenate([grad_w_qkv.astype(BF16), grad_w_out.astype(BF16)], axis=1)
        qkv_sums = jnp.sum(grad_qkv_low.astype(F32), axis=0).reshape(3, col_width)
        own_sums = jnp.concatenate(
            [
                qkv_sums[0],
                qkv_sums[2],
                jnp.sum(pre_low.astype(F32), axis=0),
                jnp.zeros((width - 2 * col_width - hidden_width,), F32),
            ]
        )
        small_list[at] = jnp.concatenate(
            [sums_one[:3], sums_two[:3], own_sums[None], jnp.zeros((1, width), F32)]
        )
        if at > 0:
            grad_second, sums_two, down_full, attention_grads[at], hidden_grads[at] = group_call(
                "backward", 7, (branch, grad_first, stored[at - 1][9], stored[at - 1][14]),
                (row_kind, sum_kind), "scatter", own_grads, (hidden_grads[at],),
            )
        else:
            g_tokens, attention_grads[at], small, hidden_grads[at] = end(
                branch, grad_first, own_grads, jnp.concatenate(small_list), hidden_grads[at]
            )

    attention_grads = jnp.stack(attention_grads).astype(F32)
    hidden_grads = jnp.stack(hidden_grads).astype(F32)
    small = small.reshape(8, layers, 8, width)
    sums = jnp.sum(small[:, :, :6], axis=0)
    own_sums = small[:, :, 6].transpose(1, 0, 2)
    g_b_qv = jnp.stack(
        [own_sums[:, :, :col_width], own_sums[:, :, col_width : 2 * col_width]], axis=1
    )
    g_b_in = own_sums[:, :, 2 * col_width : 2 * col_width + hidden_width]
    return (
        encoded,
        g_tokens,
        attention_grads[:, :, :cut_out].reshape(layers, kept, 3, col_width),
        g_b_qv.reshape(layers, 2, width),
        attention_grads[:, :, cut_out:].transpose(0, 2, 1),
        sums[:, 2],
        hidden_grads[:, :, :cut_down],
        g_b_in.reshape(layers, -1),
        hidden_grads[:, :, cut_down:].transpose(0, 2, 1),
        sums[:, 5],
        jnp.stack([sums[:, 0], sums[:, 3]], axis=1),
        jnp.stack([sums[:, 1], sums[:, 4]], axis=1),
    )


def solution(mesh):
    placed = (
        P(("dp", "tensor"), None),
        P("dp", None),
        P(None, "dp", None, "tensor"),
        P(),
        P(None, "tensor", "dp"),
        P(),
        P(None, "dp", "tensor"),
        P(),
        P(None, "tensor", "dp"),
        P(),
        P(),
        P(),
        P(("dp", "tensor"), None),
    )
    return jax.shard_map(
        shards,
        mesh=mesh,
        in_specs=placed,
        out_specs=(
            P(("dp", "tensor"), None),
            P(("dp", "tensor"), None),
            P(None, "dp", None, "tensor"),
            P(),
            P(None, "tensor", "dp"),
            P(),
            P(None, "dp", "tensor"),
            P(),
            P(None, "tensor", "dp"),
            P(),
            P(),
            P(),
        ),
        check_vma=False,
    )
```

profile of v0, /device:TPU:1, one launch (start us, length us, event | category | flops | bytes accessed | tf_op | source)
XLA Modules:
  0.0 392.7 jit_solution(10548171293464958020)
XLA Ops:
  9.2 26.8 %start.1 = (bf16[8,128,1024]{2,1,0:T(8,128)(2,1)S(1)}, bf16[16,64,512]{2,1,0:T(8,128)(2,1)S(1)}, s32[8,128]{1,0:T(8,128)S(1)}, bf16[64,1024]{1,0:T(8,128)(2,1)S(1)}) custom-call(bf16[128,1024]{1,0:T(8,128)(2,1)S(1)} %copy-done.3, bf16[64,512]{1,0:T(8,128)(2,1)S(1)} %pad_maximum_fusion.6.weights, s32[8,128]{1,0:T(8,128)S(1)} %pad.4.lengths, ...), custom_call_target="tpu_custom_call" | custom-call | tf_op jit(solution)/shard_map/start/pallas_call | solution.py:536
  36.0 1.3 copy-done.12
  38.7 2.6 add_convert_fusion.3
  42.0 1.9 fusion.75
  43.9 1.1 fusion
  45.1 1.5 fusion.35
  47.2 2.1 convolution_convert_fusion.7
  49.3 34.0 %forward2.1 = (f32[128,1024]{1,0:T(8,128)S(1)}, f32[128,1024]{1,0:T(8,128)S(1)}, bf16[8,128,1024]{2,1,0:T(8,128)(2,1)S(1)}, bf16[16,64,1024]{2,1,0:T(8,128)(2,1)...) custom-call(bf16[8,128,1024]{2,1,0:T(8,128)(2,1)} %bitcast.272, ...), custom_call_target="tpu_custom_call" | custom-call | tf_op jit(solution)/shard_map/forward2/pallas_call | solution.py:670
  83.3 8.9 %multiply_convert_fusion.3 = (bf16[1024,512]{1,0:T(8,128)(2,1)S(1)}, f32[1024,512]{1,0:T(8,128)}, f32[1024,512]{1,0:T(8,128)}) fusion(f32[512]{0:T(512)S(1)} %bitcast.320, bf16[1024,1024]{1,0:T(8,128)(2,1)S(1)} %bitcast.258, bf16[1024,1024]{1,0:T(8,128)(2,1)} %bitcast.325), kind=kOutput, calls=%fused_computation.45 | convolution fusion | flops 1108344832 | bytes 8390656 | tf_op jit(solution)/shard_map/dot_general | solution.py:925
  92.2 1.3 convolution_convert_fusion.5
  93.5 30.6 %forward4.1 = (f32[128,1024]{1,0:T(8,128)S(1)}, f32[128,1024]{1,0:T(8,128)S(1)}, bf16[8,128,1024]{2,1,0:T(8,128)(2,1)S(1)}, bf16[16,64,1536]{2,1,0:T(8,128)(2,1)}) custom-call(bf16[8,128,1024]{2,1,0:T(8,128)(2,1)S(1)} %bitcast.240, f32[128,1024]{1,0:T(8,128)S(1)} %get-tuple-element.58.refs_1_, f32[8,1024]{1,0:T(8,128)S(1)} %stack.82.refs_2_, ...), custom_call_target="tpu_custom_call" | custom-call | tf_op jit(solution)/shard_map/forward4/pallas_call | solution.py:670
  124.2 2.8 add_convert_fusion.2
  126.9 1.9 fusion.76
  128.9 1.1 fusion.1
  130.0 2.1 copy-done.21
  132.1 1.5 fusion.34
  134.8 24.7 %forward3.1 = (f32[128,1024]{1,0:T(8,128)S(1)}, f32[128,1024]{1,0:T(8,128)S(1)}, bf16[8,128,1024]{2,1,0:T(8,128)(2,1)S(1)}) custom-call(bf16[8,128,1024]{2,1,0:T(8,128)(2,1)S(1)} %bitcast.236, f32[128,1024]{1,0:T(8,128)S(1)} %get-tuple-element.62.refs_1_, f32[8,1024]{1,0:T(8,128)S(1)} %stack.83.refs_2_), custom_call_target="tpu_custom_call" | custom-call | tf_op jit(solution)/shard_map/forward3/pallas_call | solution.py:670
  159.5 7.3 %multiply_convert_fusion.2 = (bf16[1024,512]{1,0:T(8,128)(2,1)S(1)}, f32[1024,512]{1,0:T(8,128)}, f32[1024,512]{1,0:T(8,128)}) fusion(f32[512]{0:T(512)S(1)} %bitcast.322, bf16[1024,1024]{1,0:T(8,128)(2,1)S(1)} %bitcast.262, bf16[1024,1536]{1,0:T(8,128)(2,1)S(1)} %bitcast.310), kind=kOutput, calls=%fused_computation.32 | convolution fusion | flops 1108344832 | bytes 8390656 | tf_op jit(solution)/shard_map/dot_general | solution.py:925
  166.8 1.3 convolution_convert_fusion.4
  168.1 24.6 %turn5.1 = (bf16[128,1024]{1,0:T(8,128)(2,1)S(1)}, f32[128,1024]{1,0:T(8,128)S(1)}, f32[8,1024]{1,0:T(8,128)S(1)}, bf16[8,128,1024]{2,1,0:T(8,128)(2,1)S(1)}) custom-call(bf16[8,128,1024]{2,1,0:T(8,128)(2,1)S(1)} %bitcast.239, f32[128,1024]{1,0:T(8,128)S(1)} %get-tuple-element.64.refs_1_, f32[8,1024]{1,0:T(8,128)S(1)} %stack.84.refs_2_, ...), custom_call_target="tpu_custom_call" | custom-call | tf_op jit(solution)/shard_map/turn5/pallas_call | solution.py:670
  192.7 4.3 %convert_reduce_fusion = (f32[512]{0:T(512)S(1)}, bf16[1024,512]{1,0:T(8,128)(2,1)S(1)}) fusion(f32[1024,512]{1,0:T(8,128)} %get-tuple-element.133, bf16[1024,1024]{1,0:T(8,128)(2,1)S(1)} %bitcast.266, bf16[1024,1536]{1,0:T(8,128)(2,1)S(1)} %bitcast.312, f32[1024,512]{1,0:T(8,128)} %get-tuple-element.187, f32[512]{0:T(512)S(1)} %bitcast.323), kind=kOutput, calls=%fused_computation.28 | convolution fusion | flops 1082654208 | bytes 8392704 | tf_op jit(solution)/shard_map/dot_general | solution.py:956
  197.0 1.3 convolution_convert_fusion.10
  198.3 1.3 convolution_convert_fusion.11
  199.6 1.5 pad_maximum_fusion
  201.2 4.0 %copy.65 = bf16[1024,1024]{1,0:T(8,128)(2,1)} copy(bf16[1024,1024]{0,1:T(8,128)(2,1)} %pad_maximum_fusion) | data formatting | bytes 4194304 | tf_op jit(solution)/shard_map/concatenate | solution.py:967
  205.8 4.3 %convolution_convert_fusion.3 = bf16[1024,1024]{1,0:T(8,128)(2,1)} fusion(bf16[1024,512]{1,0:T(8,128)(2,1)} %copy-done.48, bf16[1024,1536]{1,0:T(8,128)(2,1)} %bitcast.306), kind=kOutput, calls=%fused_computation.64 | convolution fusion | flops 1074790400 | bytes 4194304 | tf_op jit(solution)/shard_map/dot_general | solution.py:964
  210.1 31.8 %backward8.1 = (f32[128,1024]{1,0:T(8,128)S(1)}, f32[8,1024]{1,0:T(8,128)S(1)}, bf16[8,128,1024]{2,1,0:T(8,128)(2,1)S(1)}, bf16[64,1024]{1,0:T(8,128)(2,1)S(1)}, bf16[128,1024]{1,0:T(8,128)(2,1)S(1)}) custom-call(bf16[8,128,1024]{2,1,0:T(8,128)(2,1)} %bitcast.280, f32[128,1024]{1,0:T(8,128)S(1)} %get-tuple-element.67.refs_1_, f32[8,1024]{1,0:T(8,128)S(1)} %stack.83.refs_2_, ...), custom_call_target="tpu_custom_call" | custom-call | tf_op jit(solution)/shard_map/backward8/pallas_call | solution.py:670
  242.4 1.8 convolution_convert_fusion.17
  244.8 1.4 fusion.27
  246.2 1.9 multiply_reduce_fusion.1
  248.1 2.3 multiply_convert_fusion.1
  250.5 1.4 fusion.32
  254.5 3.8 convolution_convert_fusion.1
  259.3 1.5 copy.69
  261.7 26.9 %backward7.1 = (f32[128,1024]{1,0:T(8,128)S(1)}, f32[8,1024]{1,0:T(8,128)S(1)}, bf16[8,128,1024]{2,1,0:T(8,128)(2,1)S(1)}, bf16[64,512]{1,0:T(8,128)(2,1)S(1)}, bf16[64,1024]{1,0:T(8,128)(2,1)S(1)}) custom-call(bf16[8,128,1024]{2,1,0:T(8,128)(2,1)} %bitcast.279, f32[128,1024]{1,0:T(8,128)S(1)} %get-tuple-element.72.refs_1_, f32[8,1024]{1,0:T(8,128)S(1)} %stack.82.refs_2_, ...), custom_call_target="tpu_custom_call" | custom-call | tf_op jit(solution)/shard_map/backward7/pallas_call | solution.py:670
  288.6 3.6 convert_reduce_fusion.1
  292.3 1.3 convolution_convert_fusion.8
  294.3 1.3 convolution_convert_fusion.9
  295.8 2.6 copy.70
  298.4 2.9 convolution_convert_fusion.2
  301.2 27.2 %backward6.1 = (f32[128,1024]{1,0:T(8,128)S(1)}, f32[8,1024]{1,0:T(8,128)S(1)}, bf16[8,128,1024]{2,1,0:T(8,128)(2,1)S(1)}, bf16[64,1024]{1,0:T(8,128)(2,1)S(1)}, bf16[64,512]{1,0:T(8,128)(2,1)S(1)}) custom-call(bf16[8,128,1024]{2,1,0:T(8,128)(2,1)S(1)} %bitcast.242, f32[128,1024]{1,0:T(8,128)S(1)} %get-tuple-element.76.refs_1_, ...), custom_call_target="tpu_custom_call" | custom-call | tf_op jit(solution)/shard_map/backward6/pallas_call | solution.py:670
  333.0 4.9 %fusion.24 = bf16[1024,1,2,64]{0,3,2,1:T(8,128)(2,1)S(1)} fusion(bf16[1024,2,64]{0,2,1:T(8,128)(2,1)S(1)} %bitcast.275, f32[2,1024,1024]{1,2,0:T(8,128)} %copy-done.20, f32[2,1024]{1,0:T(2,128)S(1)} %log_add_fusion.1), kind=kOutput, calls=%fused_computation.81 | convolution fusion | flops 272629760 | bytes 8921088 | tf_op jit(solution)/shard_map/hqk,qhd->khd/dot_general | solution.py:813
  338.0 4.5 %multiply_reduce_fusion = (f32[2,1024]{1,0:T(2,128)S(1)}, f32[2,1024,1024]{1,2,0:T(8,128)S(1)}) fusion(f32[2,1024,1024]{1,2,0:T(8,128)} %copy-done.20, f32[2,1024]{1,0:T(2,128)S(1)} %log_add_fusion.1, bf16[1024,2,64]{0,2,1:T(8,128)(2,1)S(1)} %bitcast.276, bf16[1024,3,2,64]{0,3,2,1:T(8,128)(2,1)S(1)} %bitcast.283), kind=kOutput, calls=%fused_computation.1 | convolution fusion | flops 274724864 | bytes 17317888 | tf_op jit(solution)/shard_map/qhd,khd->hqk/dot_general | solution.py:810
  342.6 2.5 multiply_convert_fusion
  345.1 1.4 fusion.30
  350.3 1.5 copy.74
  352.1 2.4 convolution_convert_fusion
  354.6 30.2 %end.1 = (bf16[128,1024]{1,0:T(8,128)(2,1)S(1)}, bf16[64,512]{1,0:T(8,128)(2,1)S(1)}, f32[8,16,1024]{2,1,0:T(8,128)S(1)}, bf16[64,1024]{1,0:T(8,128)(2,1)S(1)}) custom-call(bf16[8,128,1024]{2,1,0:T(8,128)(2,1)S(1)} %bitcast.241, f32[128,1024]{1,0:T(8,128)S(1)} %get-tuple-element.80.held, bf16[16,64,512]{2,1,0:T(8,128)(2,1)S(1)} %bitcast.237, ...), custom_call_target="tpu_custom_call" | custom-call | tf_op jit(solution)/shard_map/end/pallas_call | solution.py:754
  (193 shorter events, 35.2 us)
Async XLA Ops:
  0.6 8.5 %copy-start.3 = (bf16[128,1024]{1,0:T(8,128)(2,1)S(1)}, bf16[128,1024]{1,0:T(8,128)(2,1)}, u32[]{:S(2)}) copy-start(bf16[128,1024]{1,0:T(8,128)(2,1)} %tokens.1) | copy-start | bytes 786436
  4.5 2.6 copy-start.31
  37.3 9.9 %copy-start = (bf16[16,64,512]{2,1,0:T(8,128)(2,1)}, bf16[16,64,512]{2,1,0:T(8,128)(2,1)S(1)}, u32[]{:S(2)}) copy-start(bf16[16,64,512]{2,1,0:T(8,128)(2,1)S(1)} %get-tuple-element.53) | copy-start | bytes 3145732
  41.3 3.8 copy-start.22
  43.9 3.3 copy-start.20
  47.2 36.1 %copy-start.26 = (bf16[2,64,1024]{2,1,0:T(8,128)(2,1)}, bf16[2,64,1024]{2,1,0:T(8,128)(2,1)S(1)}, u32[]{:S(2)}) copy-start(bf16[2,64,1024]{2,1,0:T(8,128)(2,1)S(1)} %fusion.35) | copy-start | bytes 786436
  47.2 2.1 copy-start.2
  83.3 8.9 %copy-start.16 = (bf16[8,128,1024]{2,1,0:T(8,128)(2,1)}, bf16[8,128,1024]{2,1,0:T(8,128)(2,1)S(1)}, u32[]{:S(2)}) copy-start(bf16[8,128,1024]{2,1,0:T(8,128)(2,1)S(1)} %get-tuple-element.56) | copy-start | bytes 6291460
  83.3 8.9 %copy-start.42 = (bf16[16,64,1024]{2,1,0:T(8,128)(2,1)S(1)}, bf16[16,64,1024]{2,1,0:T(8,128)(2,1)}, u32[]{:S(2)}) copy-start(bf16[16,64,1024]{2,1,0:T(8,128)(2,1)} %get-tuple-element.57) | copy-start | bytes 6291460
  124.1 2.8 copy-start.18
  126.9 3.1 copy-start.24
  128.8 3.3 copy-start.21
  132.1 1.9 copy-start.33
  133.7 25.8 %copy-start.28 = (bf16[2,64,1024]{2,1,0:T(8,128)(2,1)}, bf16[2,64,1024]{2,1,0:T(8,128)(2,1)S(1)}, u32[]{:S(2)}) copy-start(bf16[2,64,1024]{2,1,0:T(8,128)(2,1)S(1)} %fusion.34) | copy-start | bytes 786436
  192.7 4.3 %copy-start.47 = (bf16[1024,512]{1,0:T(8,128)(2,1)S(1)}, bf16[1024,512]{1,0:T(8,128)(2,1)}, u32[]{:S(2)}) copy-start(bf16[1024,512]{1,0:T(8,128)(2,1)} %copy-done.46) | copy-start | bytes 3145732
  205.8 39.1 %slice-start.2 = ((s8[8388608]{0:T(1024)(128)(4,1)}), s8[4194304]{0:T(1024)(128)(4,1)S(1)}, s32[]{:S(2)}) async-start(s8[8388608]{0:T(1024)(128)(4,1)} %bitcast.270), calls=%async_computation.2 | async-start | bytes 8388608
  210.1 31.9 %copy-start.29 = (bf16[2,64,1024]{2,1,0:T(8,128)(2,1)S(1)}, bf16[2,64,1024]{2,1,0:T(8,128)(2,1)}, u32[]{:S(2)}) copy-start(bf16[2,64,1024]{2,1,0:T(8,128)(2,1)} %copy-done.28) | copy-start | bytes 786436
  210.1 34.7 %slice-start.3 = ((s8[8388608]{0:T(1024)(128)(4,1)}), s8[4194304]{0:T(1024)(128)(4,1)S(1)}, s32[]{:S(2)}) async-start(s8[8388608]{0:T(1024)(128)(4,1)} %bitcast.270), calls=%async_computation.3 | async-start | bytes 8388608
  241.9 2.3 copy-start.4
  244.8 1.4 copy-start.25
  251.9 1.6 copy-start.19
  261.7 26.9 %copy-start.43 = (bf16[16,64,1024]{2,1,0:T(8,128)(2,1)S(1)}, bf16[16,64,1024]{2,1,0:T(8,128)(2,1)}, u32[]{:S(2)}) copy-start(bf16[16,64,1024]{2,1,0:T(8,128)(2,1)} %get-tuple-element.57) | copy-start | bytes 6291460
  261.7 26.9 %copy-start.50 = (f32[1024,512]{1,0:T(8,128)S(1)}, f32[1024,512]{1,0:T(8,128)}, u32[]{:S(2)}) copy-start(f32[1024,512]{1,0:T(8,128)} %get-tuple-element.135) | copy-start | bytes 6291460
  288.6 3.7 copy-start.6
  288.6 3.7 copy-start.10
  288.6 3.7 copy-start.14
  288.6 3.7 copy-start.45
  292.3 2.0 copy-start.17
  298.4 2.9 copy-start.11
  301.2 27.3 %copy-start.27 = (bf16[2,64,1024]{2,1,0:T(8,128)(2,1)S(1)}, bf16[2,64,1024]{2,1,0:T(8,128)(2,1)}, u32[]{:S(2)}) copy-start(bf16[2,64,1024]{2,1,0:T(8,128)(2,1)} %copy-done.26) | copy-start | bytes 786436
  328.5 2.1 copy-start.8
  328.5 2.1 copy-start.39
  328.5 2.7 copy-start.38
  328.6 3.9 copy-start.15
  333.0 4.9 %copy-start.23 = (bf16[1024,384]{0,1:T(8,128)(2,1)S(1)}, bf16[1024,384]{0,1:T(8,128)(2,1)}, u32[]{:S(2)}) copy-start(bf16[1024,384]{0,1:T(8,128)(2,1)} %copy-done.22) | copy-start | bytes 2359300
  333.0 9.5 %slice-start = ((s8[8388608]{0:T(1024)(128)(4,1)}), s8[4194304]{0:T(1024)(128)(4,1)S(1)}, s32[]{:S(2)}) async-start(s8[8388608]{0:T(1024)(128)(4,1)} %bitcast.268), calls=%async_computation | async-start | bytes 8388608
  338.0 4.6 %slice-start.1 = ((s8[8388608]{0:T(1024)(128)(4,1)}), s8[4194304]{0:T(1024)(128)(4,1)S(1)}, s32[]{:S(2)}) async-start(s8[8388608]{0:T(1024)(128)(4,1)} %bitcast.268), calls=%async_computation.1 | async-start | bytes 8388608
  346.5 1.6 copy-start.13
  347.6 1.6 copy-start.30
  349.1 2.9 copy-start.40
  349.1 2.8 copy-start.41
  349.1 2.9 copy-start.32
  349.2 2.8 copy-start.34
  349.2 2.8 copy-start.35
  349.2 2.8 copy-start.36
  349.2 2.8 copy-start.37
  351.8 2.8 copy-start.9
  354.6 35.4 %copy-start.7 = (bf16[64,1024]{1,0:T(8,128)(2,1)S(1)}, bf16[64,1024]{1,0:T(8,128)(2,1)}, u32[]{:S(2)}) copy-start(bf16[64,1024]{1,0:T(8,128)(2,1)} %copy-done.6) | copy-start | bytes 393220
  (7 other events, 8.8 us)
where the time goes:
time: 400 us; the launch traced here: 393 us
  Pallas kernels  257 us (64%)
  matrix products  83 us (21%)
  local copies, waits for them, and re-layouts  32.3 us (8%)
  other arithmetic  18.4 us (5%)
    pallas_call x7, Pallas kernels, group_call(): pl.pallas_call(kernel, out_shape=shapes, in_specs=[VMEM] * len(given), ou...  200 us
    pallas_call x1, Pallas kernels, end(): pl.pallas_call(end_kernel, out_shape=(jax.ShapeDtypeStruct((rows, width),...  30.2 us
    pallas_call x1, Pallas kernels, start(): pl.pallas_call(start_kernel, out_shape=(jax.ShapeDtypeStruct((8, rows, wi...  26.8 us
    dot_general x2, matrix products, shards(): pre_gelu = jnp.dot(mlp_input, full_in, preferred_element_type=F32) + bias_in  16.3 us
    unnamed x118, local copies, waits for them, and re-layouts  10.9 us

commit v1 on v0

v1 whole, which is shorter than its diff:
```python
import functools
import types

import jax
import jax.numpy as jnp
from jax import lax
from jax.experimental import pallas as pl
from jax.experimental.pallas import tpu as pltpu
from jax.sharding import PartitionSpec as P

DH = 64
EPSILON = 1e-06
MESH = pl.DeviceIdType.MESH
F32 = jnp.float32
BF16 = jnp.bfloat16


def place():
    dp, tensor = lax.axis_index("dp"), lax.axis_index("tensor")
    core = lax.rem(dp, 2)
    z = lax.rem(lax.div(dp, 2), 4)
    x = lax.rem(lax.div(tensor, 4) * 2 + lax.div(dp, 8), 4)
    y = lax.rem(tensor, 4)
    return x, y, z, core


def device(x, y, z, core):
    x, y, z = lax.rem(x, 4), lax.rem(y, 4), lax.rem(z, 4)
    return (lax.rem(x, 2) * 8 + z * 2 + core, lax.div(x, 2) * 4 + y)


def block_of(x, z):
    x, z = lax.rem(x, 4), lax.rem(z, 4)
    return lax.rem(x, 2) * 8 + z * 2 + lax.div(x, 2)


def greet(devices):
    barrier = pltpu.get_barrier_semaphore()
    for other in devices:
        pl.semaphore_signal(barrier, inc=1, device_id=other, device_id_type=MESH)
    pl.semaphore_wait(barrier, len(devices))


class Copies:
    def __init__(self, send, recv):
        self.send, self.recv, self.started = send, recv, []

    def start(self, src, dst, to):
        at = len(self.started)
        copy = pltpu.make_async_remote_copy(
            src_ref=src,
            dst_ref=dst,
            send_sem=self.send.at[at],
            recv_sem=self.recv.at[at],
            device_id=to,
            device_id_type=MESH,
        )
        copy.start()
        self.started.append(copy)
        return copy

    def wait_sends(self):
        for copy in self.started:
            copy.wait_send()


def group_neighbours():
    x, y, z, core = place()
    return (
        device(x, y, z, 1 - core),
        device(x, y + 1, z, core),
        device(x, y + 3, z, core),
    )


GATHER_COPIES = 24
SCATTER_COPIES = 20


class Gather:
    def __init__(self, copies, out, base, count):
        self.x, self.y, self.z, self.core = place()
        self.pair, self.after, self.before = group_neighbours()
        half = count // 2
        self.top, self.low = pl.ds(base, half), pl.ds(base + half, half)
        self.both = pl.ds(base, count)
        self.copies, self.out = copies, out

    def send(self, step, rows, to):
        ref = self.out.at[self.core * 4 + lax.rem(self.y + step, 4), rows]
        return self.copies.start(ref, ref, to)

    def f(self, low=None):
        if low is not None:
            self.out[self.core * 4 + self.y, self.both] = low
        self.top_after = self.send(0, self.top, self.after)
        self.low_before = self.send(0, self.low, self.before)

    def f2(self):
        self.low_after = self.send(0, self.low, self.after)
        self.top_before = self.send(0, self.top, self.before)

    def f3(self):
        self.paired = [self.send(0, self.both, self.pair)]

    def g(self):
        self.top_after.wait_recv()
        self.far_top = self.send(3, self.top, self.after)
        self.low_before.wait_recv()
        self.far_low = self.send(1, self.low, self.before)

    def h(self):
        self.low_after.wait_recv()
        self.paired.append(self.send(3, self.both, self.pair))
        self.top_before.wait_recv()
        self.paired.append(self.send(1, self.both, self.pair))

    def i(self):
        self.far_top.wait_recv()
        self.paired.append(self.send(2, self.top, self.pair))
        self.far_low.wait_recv()
        self.paired.append(self.send(2, self.low, self.pair))

    def j(self):
        for copy in self.paired:
            copy.wait_recv()


class Scatter:
    def __init__(self, copies, part, bufs, base, count):
        self.x, self.y, self.z, self.core = place()
        self.pair, self.after, self.before = group_neighbours()
        half = count // 2
        self.top, self.low = pl.ds(base, half), pl.ds(base + half, half)
        self.both = pl.ds(base, count)
        self.copies, self.part = copies, part
        self.from_pair, self.staged, self.far, self.near = bufs
        self.swaps = []

    STEPS = (2, 1, 3, 0)

    def swap(self, slot):
        at = (1 - self.core) * 4 + lax.rem(self.y + self.STEPS[slot], 4)
        src, dst = self.part.at[at, self.both], self.from_pair.at[slot, self.both]
        self.swaps.append(self.copies.start(src, dst, self.pair))

    def chip(self, slot, rows):
        own = self.part[self.core * 4 + lax.rem(self.y + self.STEPS[slot], 4), rows]
        return own.astype(F32) + self.from_pair[slot, rows].astype(F32)

    def pass_on(self, slot, rows, value, dst, to):
        self.staged[slot, rows] = value.astype(BF16)
        return self.copies.start(self.staged.at[slot, rows], dst, to)

    def a0(self):
        self.swap(0)

    def a1(self):
        for slot in (1, 2, 3):
            self.swap(slot)

    def b(self):
        self.swaps[0].wait_recv()
        top, low = self.top, self.low
        self.far_top = self.pass_on(0, top, self.chip(0, top), self.far.at[top], self.after)
        self.far_low = self.pass_on(0, low, self.chip(0, low), self.far.at[low], self.before)

    def c(self):
        top, low = self.top, self.low
        self.swaps[1].wait_recv()
        low_after = self.pass_on(1, low, self.chip(1, low), self.near.at[0, low], self.after)
        self.swaps[2].wait_recv()
        top_before = self.pass_on(2, top, self.chip(2, top), self.near.at[1, top], self.before)
        self.last = [low_after, top_before]

    def d(self):
        top, low = self.top, self.low
        self.far_top.wait_recv()
        value = self.chip(1, top) + self.far[top].astype(F32)
        self.last.append(self.pass_on(1, top, value, self.near.at[0, top], self.after))
        self.far_low.wait_recv()
        value = self.chip(2, low) + self.far[low].astype(F32)
        self.last.append(self.pass_on(2, low, value, self.near.at[1, low], self.before))

    def e(self):
        self.swaps[3].wait_recv()
        own = self.chip(3, self.both)
        for copy in self.last:
            copy.wait_recv()
        return own + self.near[0, self.both].astype(F32) + self.near[1, self.both].astype(F32)


OPENING = (
    "Aa0", "Ab", "Ba0", "Aa1", "Bb", "t", "Ac", "Ad", "t", "Ba1",
    "Bc", "Bd", "t",
)
MIDDLE = (
    "x", "x", "Ae", "Af", "Af2", "x", "x", "Be", "Bf", "Bf3",
    "Af3", "t", "Bf2", "x", "x", "Ag", "t", "Bg", "Bh", "x",
    "x", "t", "Ah", "Ai", "Aj",
)
TURN_ONE = (
    "Aw0", "+Aa0", "Bi", "+Aa1", "Aw1", "t", "+Ab", "Bj", "Bw0", "+Ba0",
)
TURN_TWO = (
    "t", "+Ac", "Bw1", "+Bb", "t", "+Ad", "+Ba1", "+Bc", "+Bd", "t",
)
CLOSING = (
    "Bi", "t", "Bj",
)


def run_chain(scatter, gather, stages, tick, before_work, after_work=None):
    x, y, z, core = place()
    count = stages[0]["part"].shape[1] // 2

    def steps_of(stage):
        return {
            half: (
                Scatter(scatter, stage["part"], stage["bufs"], at * count, count),
                Gather(gather, stage["rows"], at * count, count),
            )
            for at, half in enumerate("AB")
        }

    def run(order, stage, now, then=None):
        for name in order:
            if name == "t":
                tick()
                continue
            if name == "x":
                if stage.get("side"):
                    stage["side"].pop(0)()
                continue
            if name[0] == "+":
                steps, name = then, name[1:]
            else:
                steps = now
            half, name = name[0], name[1:]
            rows = pl.ds("AB".index(half) * count, count)
            own_scatter, own_gather = steps[half]
            if name == "e":
                stage[half] = own_scatter.e()
            elif name == "f":
                own_gather.f(stage["between"](stage[half], rows))
            elif name in ("w0", "w1"):
                blocks = pl.ds((core if name == "w1" else 1 - core) * 4, 4)
                stage["work"](blocks, rows)
            elif hasattr(own_scatter, name):
                getattr(own_scatter, name)()
            else:
                getattr(own_gather, name)()

    now = steps_of(stages[0])
    run(OPENING, stages[0], now)
    for at, stage in enumerate(stages):
        run(MIDDLE, stage, now)
        if at == len(stages) - 1:
            run(CLOSING, stage, now)
            break
        if at == 0:
            before_work()
        then = steps_of(stages[at + 1])
        run(TURN_ONE, stage, now, then)
        run(TURN_TWO, stage, now, then)
        if after_work is not None:
            after_work(at)
        now = then


def gather_all(gather, rows_out, tick, arrivals):
    count = rows_out.shape[1] // 2
    halves = [Gather(gather, rows_out, at * count, count) for at in (0, 1)]
    for half, arrive in zip(halves, arrivals):
        arrive()
        for name in ("f", "f2", "f3"):
            getattr(half, name)()
    for name in ("g", "h", "i", "j"):
        tick()
        for half in halves:
            getattr(half, name)()
        tick()


def scatter_all(scatter, part, bufs, tick):
    count = part.shape[1] // 2
    first, second = [Scatter(scatter, part, bufs, at * count, count) for at in (0, 1)]
    for name in OPENING:
        if name == "t":
            tick()
        else:
            getattr(first if name[0] == "A" else second, name[1:])()
    return first.e(), second.e()


def scatter_scratch(rows, width):
    return [
        pltpu.VMEM((4, rows, width), BF16),
        pltpu.VMEM((3, rows, width), BF16),
        pltpu.VMEM((rows, width), BF16),
        pltpu.VMEM((2, rows, width), BF16),
    ]


def sems(count):
    return [pltpu.SemaphoreType.DMA((count,)), pltpu.SemaphoreType.DMA((count,))]


def plane_ring(axis):
    x, y, z, core = place()
    if axis == "x":
        return device(x + 1, y, z, core), device(x + 3, y, z, core)
    return device(x, y, z + 1, core), device(x, y, z + 3, core)


def plane_at(first, u, v):
    return block_of(u, v) if first == "x" else block_of(v, u)


PLANE_GATHER_COPIES = 36
PLANE_SCATTER_COPIES = 36


def gather_plane(copies, out):
    x, y, z, core = place()
    quarter = out.shape[1] // 4
    paths = []
    for first, base in (("x", 0), ("z", 2 * quarter)):
        v, u = (x, z) if first == "x" else (z, x)
        other = "z" if first == "x" else "x"
        paths.append(
            types.SimpleNamespace(
                first=first,
                v=v,
                u=u,
                ring=plane_ring(first),
                cross=plane_ring(other),
                halves=(pl.ds(base, quarter), pl.ds(base + quarter, quarter)),
                whole=pl.ds(base, 2 * quarter),
            )
        )

    def send(path, dv, du, rows, to):
        at = plane_at(path.first, path.v + dv, path.u + du)
        return copies.start(out.at[at, rows], out.at[at, rows], to)

    for path in paths:
        after, before = path.ring
        top, low = path.halves
        path.ta = send(path, 0, 0, top, after)
        path.lb = send(path, 0, 0, low, before)
        path.la = send(path, 0, 0, low, after)
        path.tb = send(path, 0, 0, top, before)
        path.c = {0: [send(path, 0, 0, path.whole, to) for to in path.cross]}
    yield
    for path in paths:
        path.ta.wait_recv()
        path.ft = send(path, 3, 0, path.halves[0], path.ring[0])
        path.lb.wait_recv()
        path.fl = send(path, 1, 0, path.halves[1], path.ring[1])
    yield
    for path in paths:
        path.la.wait_recv()
        path.c[3] = [send(path, 3, 0, path.whole, to) for to in path.cross]
        path.tb.wait_recv()
        path.c[1] = [send(path, 1, 0, path.whole, to) for to in path.cross]
    last = []
    for path in paths:
        path.c[0][0].wait_recv()
        last.append(send(path, 0, 3, path.whole, path.cross[0]))
    yield
    for path in paths:
        path.ft.wait_recv()
        path.fl.wait_recv()
        path.c[2] = [send(path, 2, 0, path.whole, to) for to in path.cross]
    yield
    for path in paths:
        path.c[3][0].wait_recv()
        last.append(send(path, 3, 3, path.whole, path.cross[0]))
        path.c[1][1].wait_recv()
        last.append(send(path, 1, 1, path.whole, path.cross[1]))
    yield
    for path in paths:
        path.c[2][1].wait_recv()
        last.append(send(path, 2, 1, path.whole, path.cross[1]))
    yield
    for path in paths:
        for copy in (path.c[0][1], path.c[3][1], path.c[1][0], path.c[2][0]):
            copy.wait_recv()
    for copy in last:
        copy.wait_recv()


def scatter_plane_scratch(rows, width):
    half = rows // 2
    return [
        pltpu.VMEM((2, 4, half, width), BF16),
        pltpu.VMEM((2, 2, 4, half, width), BF16),
        pltpu.VMEM((2, 4, half, width), BF16),
        pltpu.VMEM((2, 4, half, width), BF16),
        pltpu.VMEM((2, half, width), BF16),
        pltpu.VMEM((2, 2, half, width), BF16),
        pltpu.VMEM((2, 2, half // 2, width), BF16),
    ]


def scatter_plane(copies, part, out, far, near, passed, summed, far2, near2, passed2):
    x, y, z, core = place()
    half = part.shape[1] // 2
    quarter = half // 2
    paths = []
    for at, (first, base) in enumerate((("x", 0), ("z", half))):
        u, v = (x, z) if first == "x" else (z, x)
        other = "z" if first == "x" else "x"
        paths.append(
            types.SimpleNamespace(
                at=at,
                first=first,
                u=u,
                v=v,
                ring=plane_ring(first),
                cross=plane_ring(other),
                rows=pl.ds(base, half),
                base=base,
            )
        )

    def source(path, du, v):
        return (plane_at(path.first, path.u + du, v), path.rows)

    for path in paths:
        at, (after, before) = path.at, path.ring
        path.far = [
            copies.start(
                part.at[source(path, 2, v)], far.at[at, v], after if v < 2 else before
            )
            for v in range(4)
        ]
    for path in paths:
        at, (after, before) = path.at, path.ring
        path.near = [
            copies.start(part.at[source(path, 1, v)], near.at[at, 0, v], after) for v in (2, 3)
        ] + [
            copies.start(part.at[source(path, 3, v)], near.at[at, 1, v], before) for v in (0, 1)
        ]
    yield
    for path in paths:
        at, (after, before) = path.at, path.ring
        for v in (0, 2, 1, 3):
            path.far[v].wait_recv()
            du, slot, to = (1, 0, after) if v < 2 else (3, 1, before)
            own = part[source(path, du, v)].astype(F32)
            passed[at, v] = (own + far[at, v].astype(F32)).astype(BF16)
            path.near.append(copies.start(passed.at[at, v], near.at[at, slot, v], to))
    yield
    for path in paths:
        at = path.at
        for copy in path.near:
            copy.wait_recv()
        for v in range(4):
            own = part[source(path, 0, v)].astype(F32)
            summed[at, v] = (
                own + near[at, 0, v].astype(F32) + near[at, 1, v].astype(F32)
            ).astype(BF16)
        v, (after, before) = path.v, path.cross
        top, low = pl.ds(0, quarter), pl.ds(quarter, quarter)
        v1, v2, v3 = lax.rem(v + 1, 4), lax.rem(v + 2, 4), lax.rem(v + 3, 4)
        path.ft = copies.start(summed.at[at, v2, top], far2.at[at, top], after)
        path.fl = copies.start(summed.at[at, v2, low], far2.at[at, low], before)
        path.last = [
            copies.start(summed.at[at, v1, low], near2.at[at, 0, low], after),
            copies.start(summed.at[at, v3, top], near2.at[at, 1, top], before),
        ]
    yield
    for path in paths:
        at, v, (after, before) = path.at, path.v, path.cross
        top, low = pl.ds(0, quarter), pl.ds(quarter, quarter)
        v1, v3 = lax.rem(v + 1, 4), lax.rem(v + 3, 4)
        path.ft.wait_recv()
        passed2[at, 0] = (summed[at, v1, top].astype(F32) + far2[at, top].astype(F32)).astype(BF16)
        path.last.append(copies.start(passed2.at[at, 0], near2.at[at, 0, top], after))
        path.fl.wait_recv()
        passed2[at, 1] = (summed[at, v3, low].astype(F32) + far2[at, low].astype(F32)).astype(BF16)
        path.last.append(copies.start(passed2.at[at, 1], near2.at[at, 1, low], before))
    yield
    for path in paths:
        at, v = path.at, path.v
        for copy in path.last:
            copy.wait_recv()
        total = summed[at, v].astype(F32) + near2[at, 0].astype(F32) + near2[at, 1].astype(F32)
        out[path.rows] = total.astype(out.dtype)


def params(number):
    return pltpu.CompilerParams(
        collective_id=number, has_side_effects=True, vmem_limit_bytes=56 * 2**20
    )


VMEM = pl.BlockSpec(memory_space=pltpu.VMEM)
HBM = pl.BlockSpec(memory_space=pl.ANY)


def neighbours():
    return [*group_neighbours(), *plane_ring("x"), *plane_ring("z")]


def drain(steps):
    for _ in steps:
        pass


def swap_partner():
    x, y, z, core = place()
    upper = lax.div(x, 2)
    return core != upper, device(core * 2 + lax.rem(x, 2), y, z, upper)


def greet_with_partner(others):
    moves, partner = swap_partner()
    barrier = pltpu.get_barrier_semaphore()
    for other in others:
        pl.semaphore_signal(barrier, inc=1, device_id=other, device_id_type=MESH)

    @pl.when(moves)
    def _():
        pl.semaphore_signal(barrier, inc=1, device_id=partner, device_id_type=MESH)

    pl.semaphore_wait(barrier, len(others) + moves.astype(jnp.int32))


def partner_copy(src, dst, send, recv):
    return pltpu.make_async_remote_copy(
        src_ref=src,
        dst_ref=dst,
        send_sem=send,
        recv_sem=recv,
        device_id=swap_partner()[1],
        device_id_type=MESH,
    )


class Swaps:
    def __init__(self, send, recv):
        self.send, self.recv, self.moves = send, recv, []

    def copy(self, src, dst, own_dst=None):
        at = len(self.moves)
        copy = partner_copy(src, dst, self.send.at[at], self.recv.at[at])
        self.moves.append(copy)
        moves, _ = swap_partner()

        @pl.when(moves)
        def _():
            copy.start()

        @pl.when(jnp.logical_not(moves))
        def _():
            target = dst if own_dst is None else own_dst
            target[...] = src[...]

        return copy

    def arrive(self, copy):
        @pl.when(swap_partner()[0])
        def _():
            copy.wait_recv()

    def finish(self, *arrived):
        @pl.when(swap_partner()[0])
        def _():
            for copy in self.moves:
                copy.wait_send()
                if not any(copy is other for other in arrived):
                    copy.wait_recv()


def start_kernel(
    tokens, attention, hidden, lengths, rows_out, weights_out, attention_out, hidden_out, lengths_out,
    ssend, srecv, send, recv, wsend, wrecv,
):
    x, y, z, core = place()
    greet_with_partner(neighbours())
    plane, group, swaps = Copies(wsend, wrecv), Copies(send, recv), Swaps(ssend, srecv)
    there = block_of(core * 2 + lax.rem(x, 2), z)
    own = weights_out.at[block_of(x, z)]
    weights_move = swaps.copy(attention.at[0], weights_out.at[there], own)
    count = tokens.shape[0] // 2
    rows_moves = []
    for half in (pl.ds(0, count), pl.ds(count, count)):
        own = rows_out.at[core * 4 + y, half]
        target = rows_out.at[lax.div(x, 2) * 4 + y, half]
        rows_moves.append(swaps.copy(tokens.at[half], target, own))
    swaps.copy(lengths, lengths_out)
    swaps.arrive(weights_move)
    steps = gather_plane(plane, weights_out)
    next(steps)
    arrivals = [functools.partial(swaps.arrive, move) for move in rows_moves]
    ticks = []

    def tick():
        ticks.append(None)
        next(steps, None)
        if len(ticks) == 3:
            swaps.copy(hidden, hidden_out)
            swaps.copy(attention.at[1], attention_out)

    gather_all(group, rows_out, tick, arrivals)
    drain(steps)
    swaps.finish(weights_move, *rows_moves)
    group.wait_sends()
    plane.wait_sends()


def start(tokens, attention, hidden, lengths):
    rows, width = tokens.shape
    _, held, columns = attention.shape
    shape = jax.ShapeDtypeStruct
    return pl.pallas_call(
        start_kernel,
        out_shape=(
            shape((8, rows, width), BF16),
            shape((16, held, columns), BF16),
            shape((held, columns), BF16),
            shape(hidden.shape, BF16),
            shape(lengths.shape, lengths.dtype),
        ),
        in_specs=[VMEM] * 4,
        out_specs=(VMEM,) * 5,
        scratch_shapes=sems(6) + sems(GATHER_COPIES) + sems(PLANE_GATHER_COPIES),
        compiler_params=params(0),
        name="start",
    )(tokens, attention, hidden, lengths)


def normed_parts(stream):
    row_mean = jnp.mean(stream, axis=-1, keepdims=True)
    centered = stream - row_mean
    row_var = jnp.mean(centered * centered, axis=-1, keepdims=True)
    scale = lax.rsqrt(row_var + EPSILON)
    return centered * scale, scale


def norm_pull(unit, scale, gain, grad, sums):
    scaled = grad * gain
    inner = jnp.mean(scaled * unit, axis=-1, keepdims=True)
    pulled = scale * (scaled - jnp.mean(scaled, axis=-1, keepdims=True) - unit * inner)
    low = pulled.astype(BF16)
    sums[0:1] += jnp.sum(grad * unit, axis=0, keepdims=True)
    sums[1:2] += jnp.sum(grad, axis=0, keepdims=True)
    sums[2:3] += jnp.sum(low.astype(F32), axis=0, keepdims=True)
    return pulled, low


INV_SQRT2 = 0.7071067811865476
INV_SQRT_2PI = 0.3989422804014327
CONTRACT_LAST = (((1,), (1,)), ((), ()))
CONTRACT_FIRST = (((0,), (0,)), ((), ()))


def normal_cdf(values):
    return 0.5 * (1.0 + lax.erf(values * INV_SQRT2))


def flatten(block):
    return block.reshape(block.shape[0] * block.shape[1], block.shape[2])


def hidden_forward(ref, hidden_width):
    def work(blocks, rows):
        full_in = flatten(ref.hidden_full[:, :, :hidden_width])
        full_down = flatten(ref.hidden_full[:, :, hidden_width:])
        values = flatten(ref.mlp_input[blocks, rows])
        pre_gelu = jnp.dot(values, full_in, preferred_element_type=F32) + ref.bias_in[ref.layer : ref.layer + 1]
        act = (pre_gelu * normal_cdf(pre_gelu)).astype(BF16)
        branch = lax.dot_general(act, full_down, CONTRACT_LAST, preferred_element_type=F32)
        shape = ref.mlp_input[blocks, rows].shape
        ref.pre_gelu[blocks, rows] = pre_gelu.reshape(*shape[:2], -1)
        ref.act[blocks, rows] = act.reshape(*shape[:2], -1)
        ref.branch_two[blocks, rows] = branch.astype(BF16).reshape(shape)

    return work


def hidden_backward(ref, hidden_width):
    def work(blocks, rows):
        full_in = flatten(ref.hidden_full[:, :, :hidden_width])
        full_down = flatten(ref.hidden_full[:, :, hidden_width:])
        values = flatten(ref.down_full[blocks, rows])
        grad_act = jnp.dot(values, full_down, preferred_element_type=F32)
        pre_gelu = flatten(ref.pre_gelu[blocks, rows])
        slope = normal_cdf(pre_gelu) + pre_gelu * (
            jnp.exp(pre_gelu * pre_gelu * -0.5) * INV_SQRT_2PI
        )
        low = (slope * grad_act).astype(BF16)
        branch = lax.dot_general(low, full_in, CONTRACT_LAST, preferred_element_type=F32)
        shape = ref.down_full[blocks, rows].shape
        ref.pre_low[blocks, rows] = low.reshape(*shape[:2], -1)
        ref.in_sums[0:1] += jnp.sum(low.astype(F32), axis=0, keepdims=True)
        ref.branch_three[blocks, rows] = branch.astype(BF16).reshape(shape)

    return work


def hidden_grads(ref, out):
    pieces = []
    into = out
    hidden_width = into.shape[2] // 2

    def piece(quarter, left, right, base):
        def work():
            values = flatten(left[:, :, quarter * 256 : (quarter + 1) * 256])
            grad = lax.dot_general(
                values, flatten(right[...]), CONTRACT_FIRST, preferred_element_type=F32
            )
            into[quarter * 4 : (quarter + 1) * 4, :, base : base + hidden_width] = grad.astype(
                BF16
            ).reshape(4, 64, hidden_width)

        return work

    for quarter in range(4):
        pieces.append(piece(quarter, ref.down_full, ref.act, hidden_width))
    for quarter in range(4):
        pieces.append(piece(quarter, ref.mlp_input, ref.pre_low, 0))
    return dict(side=pieces)


def param_rows(ref, at, which):
    rows = (2 * which + at, 4 + 2 * at + which, 8 + 2 * at + which)
    return [ref.params[row : row + 1] for row in rows]


def forward_norm(ref, held, at, which, stream_out, normed_out):
    def between(total, rows):
        bias, gain, shift = param_rows(ref, at, which)
        stream = held[rows].astype(F32) + total + bias
        stream_out[rows] = stream
        unit, _ = normed_parts(stream)
        normed = unit * gain + shift
        normed_out[rows] = normed
        return normed.astype(BF16)

    return between


def turn_norm(ref, held, at, which, pulled_out, sums):
    def between(total, rows):
        bias, gain, shift = param_rows(ref, at, which)
        unit, scale = normed_parts(held[rows] + total + bias)
        ref.encoded[rows] = (unit * gain + shift).astype(BF16)
        grad = ref.cotangent[rows].astype(F32)
        pulled, low = norm_pull(unit, scale, gain, grad, sums)
        pulled_out[rows] = pulled
        return low

    return between


def backward_norm(ref, held, at, which, stream, pulled_out, sums):
    def between(total, rows):
        unit, scale = normed_parts(stream[rows])
        grad = held[rows] + total
        pulled, low = norm_pull(unit, scale, param_rows(ref, at, which)[1], grad, sums)
        pulled_out[rows] = pulled
        return low

    return between


def zeroed(ref):
    if not hasattr(ref, "in_sums"):
        return ()
    return (ref.sums_one, ref.sums_two, ref.in_sums)


def chain_call(
    number, name, inputs, outputs, scratch, stages_of,
    gathers=(), scatters=(), swapped=(), late=(), early=(), pace=1, swapped_after=(),
):
    rows, width = 128, 1024
    names_in, names_out, names_scratch = list(inputs), list(outputs), list(scratch)
    stage_count = stages_of({}, True)
    shapes = []
    for key in names_out:
        shape, kind = outputs[key]
        shapes.append(jax.ShapeDtypeStruct(shape, kind))
    scratch_shapes = [pltpu.VMEM(shape, kind) for shape, kind in scratch.values()]
    for _ in range(stage_count):
        scratch_shapes += scatter_scratch(rows, width)
    scratch_shapes += sems(SCATTER_COPIES * stage_count) + sems(GATHER_COPIES * stage_count)
    pieces = [key for sources, _ in scatters for key in sources]
    stored = [key for keys, _ in early for key in keys]
    scratch_shapes += [pltpu.VMEM(inputs[key].shape, inputs[key].dtype) for key in late]
    scratch_shapes += [pltpu.VMEM(*outputs[key]) for key in stored]
    scratch_shapes += [pltpu.SemaphoreType.DMA((len(late) + len(stored) + len(pieces) + 1,))]
    for _ in gathers:
        scratch_shapes += sems(PLANE_GATHER_COPIES)
    for sources, out in scatters:
        kept, columns = {**outputs, **scratch}[out][0]
        scratch_shapes += [pltpu.VMEM((16, kept, columns), BF16)]
        scratch_shapes += sems(PLANE_SCATTER_COPIES) + scatter_plane_scratch(kept, columns)
    if swapped:
        scratch_shapes += sems(len(swapped) + len(swapped_after))

    def kernel(*refs):
        refs = list(refs)
        take = lambda count: [refs.pop(0) for _ in range(count)]
        ref = types.SimpleNamespace()
        held = vars(ref)
        for names in (names_in, names_out, names_scratch):
            held.update(zip(names, take(len(names))))
        bufs = [take(4) for _ in range(stage_count)]
        scatter, gather = Copies(*take(2)), Copies(*take(2))
        far_refs = {key: held[key] for key in (*late, *stored)}
        held.update(zip((*late, *stored), take(len(late) + len(stored))))
        (local,) = take(1)
        fetches, stores, count = [], [], []

        def local_copy(src, dst, kept):
            copy = pltpu.make_async_copy(src, dst, local.at[len(count)])
            copy.start()
            count.append(None)
            kept.append(copy)
            return copy

        for key in late:
            local_copy(far_refs[key], held[key], fetches)

        def after_work(at):
            for keys, stage in early:
                if stage == at:
                    for key in keys:
                        local_copy(held[key], far_refs[key], stores)

        x, y, z, core = place()
        others = neighbours() if gathers or scatters else group_neighbours()
        planes, queue = [], []
        for source, out in gathers:
            plane = Copies(*take(2))
            planes.append(plane)
            queue.append((gather_plane(plane, held[out]), (), True))
        for sources, out in scatters:
            (assembled,) = take(1)
            plane = Copies(*take(2))
            planes.append(plane)
            at, parts = 0, []
            for source in sources:
                columns = pl.ds(at, held[source].shape[-1])
                local_copy(held[source], assembled.at[:, :, columns], parts)
                at += held[source].shape[-1]
            steps = scatter_plane(plane, assembled, held[out], *take(7))
            queue.append((steps, parts, sources))
        stages = stages_of(ref, False)
        for stage, own in zip(stages, bufs):
            stage["bufs"] = own
        if swapped:
            swaps = Swaps(*take(2))
            greet_with_partner(others)
        else:
            greet(others)
        for sums in zeroed(ref):
            sums[...] = jnp.zeros_like(sums)
        for source, out in gathers:
            held[out][block_of(x, z)] = held[source][...]
        started, ended, ticks = [], [], [None] * (pace - 1)

        def tick():
            if not started:
                started.append(True)
                for _, parts, _ in queue:
                    for part in parts:
                        part.wait()
                for source, out in swapped:
                    swaps.copy(held[source], held[out])
            ticks.append(None)
            if len(ticks) % pace:
                return
            advance_planes()

        def advance_planes():
            while queue:
                try:
                    next(queue[0][0])
                    return
                except StopIteration:
                    queue.pop(0)
            if not ended:
                ended.append(True)
                for source, out in swapped_after:
                    swaps.copy(held[source], held[out])

        def before_work():
            if gathers and len(queue) == len(gathers) + len(scatters):
                drain(queue.pop(0)[0])
            for copy in fetches:
                copy.wait()
            fetches.clear()

        run_chain(scatter, gather, stages, tick, before_work, after_work)
        for steps, *_ in queue:
            drain(steps)
        queue.clear()
        advance_planes()
        for copies in (scatter, gather, *planes):
            copies.wait_sends()
        for copy in stores:
            copy.wait()
        if swapped:
            swaps.finish()

    results = pl.pallas_call(
        kernel,
        out_shape=tuple(shapes),
        in_specs=[HBM if key in (*late, *pieces) else VMEM for key in names_in],
        out_specs=tuple(HBM if key in stored else VMEM for key in names_out),
        scratch_shapes=scratch_shapes,
        compiler_params=params(number),
        name=name,
    )(*inputs.values())
    return dict(zip(names_out, results))


def sum_small(copies, small, out, got_x, got_z):
    x, y, z, core = place()
    own = core * 4 + y
    along_x = [device(x + step, y, z, core) for step in (1, 2, 3)]
    along_z = [device(x, y, z + step, core) for step in (1, 2, 3)]
    along_y = [device(x, y + step, z, core) for step in (1, 2, 3)]
    first = [copies.start(small, got_x.at[at], to) for at, to in enumerate(along_x)]
    yield
    for copy in first:
        copy.wait_recv()
    got_z[3] = small[...] + got_x[0] + got_x[1] + got_x[2]
    second = [copies.start(got_z.at[3], got_z.at[at], to) for at, to in enumerate(along_z)]
    yield
    for copy in second:
        copy.wait_recv()
    out[own] = got_z[3] + got_z[0] + got_z[1] + got_z[2]
    third = [copies.start(out.at[own], out.at[own], to) for to in along_y]
    yield
    for copy in third:
        copy.wait_recv()
    held = out.at[pl.ds(core * 4, 4)]
    copies.start(held, held, device(x, y, z, 1 - core)).wait_recv()


def end_kernel(*refs):
    refs = list(refs)
    take = lambda count: [refs.pop(0) for _ in range(count)]
    part, held, *pieces = take(5)
    layer_sums = [take(4), take(4)]
    rows_out, grads_out, small_out = take(3)
    grads, local = take(2)
    bufs, plane_bufs = take(4), take(7)
    rows_stage, grads_stage, small, got_x, got_z = take(5)
    swaps, group, plane, tiny = Swaps(*take(2)), Copies(*take(2)), Copies(*take(2)), Copies(*take(2))
    x, y, z, core = place()
    at, fetches = 0, []
    for number, piece in enumerate(pieces):
        columns = pl.ds(at, piece.shape[2])
        fetches.append(pltpu.make_async_copy(piece, grads.at[:, :, columns], local.at[number]))
        fetches[-1].start()
        at += piece.shape[2]
    small[...] = jnp.zeros_like(small)
    for base, (sums_one, sums_two, qkv_sums, in_sums) in zip((0, 8), layer_sums):
        third, hidden_width = qkv_sums.shape[1] // 3, in_sums.shape[1]
        small[base : base + 3] = sums_one[0:3]
        small[base + 3 : base + 6] = sums_two[0:3]
        small[base + 6 : base + 7, :third] = qkv_sums[0:1, :third]
        small[base + 6 : base + 7, third : 2 * third] = qkv_sums[0:1, 2 * third :]
        small[base + 6 : base + 7, 2 * third : 2 * third + hidden_width] = in_sums[0:1]
    greet_with_partner(
        neighbours()
        + [device(x + 2, y, z, core), device(x, y + 2, z, core), device(x, y, z + 2, core)]
    )
    tiny_steps = sum_small(tiny, small, small_out, got_x, got_z)
    plane_steps = scatter_plane(plane, grads, grads_stage, *plane_bufs)
    ticks = []

    def tick():
        ticks.append(None)
        if len(ticks) == 1:
            next(tiny_steps)
            for copy in fetches:
                copy.wait()
            next(plane_steps)
        elif len(ticks) == 2:
            next(tiny_steps)
        elif len(ticks) == 3:
            next(plane_steps)

    totals = scatter_all(group, part, bufs, tick)
    count = rows_stage.shape[0] // 2
    for at in (0, 1):
        rows = pl.ds(at * count, count)
        rows_stage[rows] = (held[rows] + totals[at]).astype(BF16)
    swaps.copy(rows_stage, rows_out)
    next(plane_steps)
    next(tiny_steps)
    next(plane_steps)
    drain(tiny_steps)
    drain(plane_steps)
    swaps.copy(grads_stage, grads_out)
    swaps.finish()
    group.wait_sends()
    plane.wait_sends()
    tiny.wait_sends()


def end(part, held, pieces, layer_sums):
    rows, width = held.shape
    kept, columns = pieces[0].shape[1], sum(piece.shape[2] for piece in pieces)
    shape = jax.ShapeDtypeStruct
    return pl.pallas_call(
        end_kernel,
        out_shape=(
            shape((rows, width), BF16),
            shape((kept, columns), BF16),
            shape((8, 16, width), F32),
        ),
        in_specs=[VMEM] * 2 + [HBM] * 3 + [VMEM] * 8,
        out_specs=(VMEM,) * 3,
        scratch_shapes=[pltpu.VMEM((16, kept, columns), BF16), pltpu.SemaphoreType.DMA((3,))]
        + scatter_scratch(rows, width)
        + scatter_plane_scratch(kept, columns)
        + [
            pltpu.VMEM((rows, width), BF16),
            pltpu.VMEM((kept, columns), BF16),
            pltpu.VMEM((16, width), F32),
            pltpu.VMEM((3, 16, width), F32),
            pltpu.VMEM((4, 16, width), F32),
        ]
        + sems(2)
        + sems(SCATTER_COPIES)
        + sems(PLANE_SCATTER_COPIES)
        + sems(10),
        compiler_params=params(1),
        name="end",
    )(part, held, *pieces, *layer_sums[0], *layer_sums[1])


def finish_kernel(
    small, zero, one,
    g_qkv, g_b_qv, g_out, g_b_out, g_in, g_b_in, g_down, g_b_down, g_gain, g_shift,
):
    third, hidden_width = g_out.shape[1], g_in.shape[2]
    cut = 4 * third
    for at, grads in enumerate((zero, one)):
        for which in range(3):
            columns = slice(which * third, (which + 1) * third)
            g_qkv[at, :, which] = grads[:, columns].astype(F32)
        g_out[at] = grads[:, 3 * third : cut].astype(F32).T
        g_in[at] = grads[:, cut : cut + hidden_width].astype(F32)
        g_down[at] = grads[:, cut + hidden_width :].astype(F32).T
        rows = jnp.sum(small[:, at * 8 : at * 8 + 8], axis=0)
        g_gain[at, 0:1], g_shift[at, 0:1], g_b_out[at : at + 1] = rows[0:1], rows[1:2], rows[2:3]
        g_gain[at, 1:2], g_shift[at, 1:2], g_b_down[at : at + 1] = rows[3:4], rows[4:5], rows[5:6]
        for block in range(8):
            row = small[block, at * 8 + 6 : at * 8 + 7]
            columns = slice(block * third, (block + 1) * third)
            g_b_qv[at, 0:1, columns] = row[:, :third]
            g_b_qv[at, 1:2, columns] = row[:, third : 2 * third]
            columns = slice(block * hidden_width, (block + 1) * hidden_width)
            g_b_in[at : at + 1, columns] = row[:, 2 * third : 2 * third + hidden_width]


def finish(small, zero, one, third):
    kept, hidden_width = zero.shape[0], (zero.shape[1] - 4 * third) // 2
    width = small.shape[2]
    shapes = (
        (2, kept, 3, third),
        (2, 2, width),
        (2, third, kept),
        (2, width),
        (2, kept, hidden_width),
        (2, 8 * hidden_width),
        (2, hidden_width, kept),
        (2, width),
        (2, 2, width),
        (2, 2, width),
    )
    return pl.pallas_call(
        finish_kernel,
        out_shape=tuple(jax.ShapeDtypeStruct(shape, F32) for shape in shapes),
        in_specs=[VMEM] * 3,
        out_specs=(VMEM,) * len(shapes),
        compiler_params=pltpu.CompilerParams(vmem_limit_bytes=48 * 2**20),
        name="finish",
    )(small, zero, one)


HEAD_SCALE = DH ** (-0.5)


def segment_parts(lengths, rows):
    def of(shape, dim):
        positions = lax.broadcasted_iota(jnp.int32, shape, dim)
        end, segments = 0, jnp.zeros(shape, jnp.int32)
        for at in range(4):
            end = end + lengths[0, at]
            segments += (positions >= end).astype(jnp.int32)
        return jnp.where(segments == 4, 4 + positions, segments)

    return of((rows, 1), 0), of((1, rows), 1)


def head_lanes(values, head):
    lanes = lax.broadcasted_iota(jnp.int32, values.shape, 1)
    return jnp.where((lanes >= head * DH) & (lanes < (head + 1) * DH), values, 0)


def pick_heads(parts):
    features = lax.broadcasted_iota(jnp.int32, parts[0].shape, 0)
    return jnp.where(features < DH, parts[0], parts[1])


CHUNK = 512


def attend_kernel(lengths, rows, weights, bias, qkv_out, context_out, lse_out, branch_out, v_turned, seg_row):
    total, width = rows.shape[0], context_out.shape[1]
    column, row = segment_parts(lengths, total)
    seg_row[...] = jnp.broadcast_to(row, seg_row.shape)

    def chunk(at):
        return pl.ds(pl.multiple_of(at * CHUNK, CHUNK), CHUNK)

    @pl.loop(0, total // CHUNK)
    def _(at):
        r = chunk(at)
        qkv = jnp.dot(rows[r], weights[:, : 3 * width], preferred_element_type=F32)
        qkv_out[r] = (qkv + bias[0:1]).astype(BF16)

    keys = qkv_out[:, width : 2 * width]
    v_turned[...] = qkv_out[:, 2 * width :].astype(F32).T.astype(BF16)

    @pl.loop(0, total // CHUNK)
    def _(at):
        r = chunk(at)
        queries = qkv_out[r, :width].astype(F32) * HEAD_SCALE
        allowed = column == seg_row[0:1, r]
        parts = []
        for head in range(2):
            own = head_lanes(queries, head).astype(BF16)
            scores = lax.dot_general(keys, own, CONTRACT_LAST, preferred_element_type=F32)
            scores = jnp.where(allowed, scores, -1e30)
            peak = jnp.max(scores, axis=0, keepdims=True)
            raised = jnp.exp(scores - peak)
            total_row = jnp.sum(raised, axis=0, keepdims=True)
            probs = (raised * (1.0 / total_row)).astype(BF16)
            parts.append(jnp.dot(v_turned[...], probs, preferred_element_type=F32))
            lse_out[head : head + 1, r] = peak + jnp.log(total_row)
        context = pick_heads(parts).T.astype(BF16)
        context_out[r] = context
        branch = lax.dot_general(
            context, weights[:, 3 * width :], CONTRACT_LAST, preferred_element_type=F32
        )
        branch_out[r] = branch.astype(BF16)


def attend(lengths, rows, weights, bias):
    total, width = rows.shape[0], weights.shape[1] // 4
    shape = jax.ShapeDtypeStruct
    return pl.pallas_call(
        attend_kernel,
        out_shape=(
            shape((total, 3 * width), BF16),
            shape((total, width), BF16),
            shape((8, total), F32),
            shape((total, rows.shape[1]), BF16),
        ),
        in_specs=[pl.BlockSpec(memory_space=pltpu.SMEM)] + [VMEM] * 3,
        out_specs=(VMEM,) * 4,
        scratch_shapes=[pltpu.VMEM((width, total), BF16), pltpu.VMEM((8, total), jnp.int32)],
        compiler_params=pltpu.CompilerParams(vmem_limit_bytes=48 * 2**20),
        name="attend",
    )(lengths, rows, weights, bias)


def attend_back_kernel(
    lengths, grad_rows, rows, weights, qkv, context, lse,
    g_qkv, g_out, branch_out, sums_out,
    grad_context, grad_qkv, k_turned, k_sum, v_sum, seg_row,
):
    total, width = rows.shape[0], context.shape[1]
    column, row = segment_parts(lengths, total)
    seg_row[...] = jnp.broadcast_to(row, seg_row.shape)

    def chunk(at):
        return pl.ds(pl.multiple_of(at * CHUNK, CHUNK), CHUNK)

    @pl.loop(0, total // CHUNK)
    def _(at):
        r = chunk(at)
        grad_context[r] = jnp.dot(
            grad_rows[r], weights[:, 3 * width :], preferred_element_type=F32
        ).astype(BF16)

    keys, values = qkv[:, width : 2 * width], qkv[:, 2 * width :]
    k_turned[...] = keys.astype(F32).T.astype(BF16)
    k_sum[...] = jnp.zeros_like(k_sum)
    v_sum[...] = jnp.zeros_like(v_sum)

    @pl.loop(0, total // CHUNK)
    def _(at):
        r = chunk(at)
        queries = qkv[r, :width].astype(F32) * HEAD_SCALE
        grads = grad_context[r].astype(F32)
        allowed = column == seg_row[0:1, r]
        parts = []
        for head in range(2):
            own = head_lanes(queries, head).astype(BF16)
            own_grads = head_lanes(grads, head).astype(BF16)
            scores = lax.dot_general(keys, own, CONTRACT_LAST, preferred_element_type=F32)
            scores = jnp.where(allowed, scores, -1e30)
            probs = jnp.exp(scores - lse[head : head + 1, r])
            grad_probs = lax.dot_general(
                values, own_grads, CONTRACT_LAST, preferred_element_type=F32
            )
            v_sum[...] += jnp.dot(probs.astype(BF16), own_grads, preferred_element_type=F32)
            inner = jnp.sum(probs * grad_probs, axis=0, keepdims=True)
            grad_scores = (probs * (grad_probs - inner)).astype(BF16)
            k_sum[...] += jnp.dot(grad_scores, own, preferred_element_type=F32)
            parts.append(jnp.dot(k_turned[...], grad_scores, preferred_element_type=F32))
        grad_qkv[r, :width] = (pick_heads(parts).T * HEAD_SCALE).astype(BF16)

    grad_qkv[:, width : 2 * width] = k_sum[...].astype(BF16)
    grad_qkv[:, 2 * width :] = v_sum[...].astype(BF16)
    sums_out[...] = jnp.broadcast_to(
        jnp.sum(grad_qkv[...].astype(F32), axis=0, keepdims=True), sums_out.shape
    )

    @pl.loop(0, total // CHUNK)
    def _(at):
        r = chunk(at)
        branch = lax.dot_general(
            grad_qkv[r], weights[:, : 3 * width], CONTRACT_LAST, preferred_element_type=F32
        )
        branch_out[r] = branch.astype(BF16)

    @pl.loop(0, rows.shape[1] // CHUNK)
    def _(at):
        c = chunk(at)
        turned = lax.dot_general(
            grad_qkv[...], rows[:, c], CONTRACT_FIRST, preferred_element_type=F32
        )
        g_qkv[c] = turned.T.astype(BF16)
        turned = lax.dot_general(
            context[...], grad_rows[:, c], CONTRACT_FIRST, preferred_element_type=F32
        )
        g_out[c] = turned.T.astype(BF16)


def attend_back(lengths, grad_rows, rows, weights, qkv, context, lse):
    total, width = context.shape
    depth = rows.shape[1]
    shape = jax.ShapeDtypeStruct
    return pl.pallas_call(
        attend_back_kernel,
        out_shape=(
            shape((depth, 3 * width), BF16),
            shape((depth, width), BF16),
            shape((total, depth), BF16),
            shape((8, 3 * width), F32),
        ),
        in_specs=[pl.BlockSpec(memory_space=pltpu.SMEM)] + [VMEM] * 6,
        out_specs=(VMEM,) * 4,
        scratch_shapes=[
            pltpu.VMEM((total, width), BF16),
            pltpu.VMEM((total, 3 * width), BF16),
            pltpu.VMEM((width, total), BF16),
            pltpu.VMEM((total, width), F32),
            pltpu.VMEM((total, width), F32),
            pltpu.VMEM((8, total), jnp.int32),
        ],
        compiler_params=pltpu.CompilerParams(vmem_limit_bytes=48 * 2**20),
        name="attend_back",
    )(lengths, grad_rows, rows, weights, qkv, context, lse)


def shards(
    tokens,
    lengths,
    w_qkv,
    b_qv,
    w_out,
    b_out,
    w_in,
    b_in,
    w_down,
    b_down,
    ln_gain,
    ln_bias,
    cotangent,
):
    x, y, z, core = place()
    column = core * 4 + y
    own_rows, width = tokens.shape
    total_rows = own_rows * 8
    layers, kept = w_qkv.shape[:2]
    col_width = w_qkv.shape[3]
    hidden_width = w_in.shape[2]

    attention_shards = jnp.concatenate(
        [w_qkv.reshape(layers, kept, 3 * col_width), w_out.transpose(0, 2, 1)], axis=2
    )
    hidden_shards = jnp.concatenate([w_in, w_down.transpose(0, 2, 1)], axis=2)
    lengths = jnp.pad(lengths, ((0, 7), (0, 128 - lengths.shape[1])))
    rows_zero, attention_zero, attention_shard, hidden_moved, lengths = start(
        tokens, attention_shards, hidden_shards, lengths
    )
    hidden = lax.dynamic_index_in_dim(rows_zero, column, 0, keepdims=False)

    norm_params = jnp.concatenate(
        [b_out, b_down, ln_gain.reshape(4, width), ln_bias.reshape(4, width)]
    ).astype(F32)
    bias_in = lax.dynamic_slice_in_dim(b_in, column * hidden_width, hidden_width, 1).astype(F32)
    bias_qv = lax.dynamic_slice_in_dim(b_qv, column * col_width, col_width, 2).astype(F32)
    bias_qkv = jnp.concatenate(
        [bias_qv[:, 0], jnp.zeros((layers, col_width), F32), bias_qv[:, 1]], axis=1
    )

    own_kind = ((own_rows, width), F32)
    sum_kind = ((8, width), F32)
    low_kind = ((own_rows, width), BF16)
    all_kind = ((8, own_rows, width), BF16)
    act_kind = ((8, own_rows, hidden_width), BF16)
    gelu_kind = ((8, own_rows, hidden_width), F32)
    in_sum_kind = ((8, hidden_width), F32)
    hidden_kind = ((16, kept, 2 * hidden_width), BF16)
    attention_kind = ((16, kept, 4 * col_width), BF16)
    grads_kind = ((kept, 4 * col_width + 2 * hidden_width), BF16)

    def attention(at, rows, full):
        rows, full = rows.reshape(total_rows, width), full.reshape(width, 4 * col_width)
        qkv, context, lse, branch = attend(lengths, rows, full, bias_qkv[at : at + 1])
        return branch.reshape(all_kind[0]), (rows, full, qkv, context, lse)

    def attention_back(stored, rows):
        grad_rows = rows.reshape(total_rows, width)
        g_qkv, g_out, branch, sums = attend_back(lengths, grad_rows, *stored)
        pieces = (g_qkv.reshape(16, kept, -1), g_out.reshape(16, kept, -1))
        return branch.reshape(all_kind[0]), pieces, sums

    branch, stored_zero = attention(0, rows_zero, attention_zero)

    def zero_stages(ref, counting):
        if counting:
            return 2
        ref.layer = 0
        return [
            dict(
                part=ref.branch,
                rows=ref.mlp_input,
                between=forward_norm(ref, ref.held, 0, 0, ref.first_sum, ref.normed),
                work=hidden_forward(ref, hidden_width),
            ),
            dict(
                part=ref.branch_two,
                rows=ref.rows,
                between=forward_norm(ref, ref.normed, 0, 1, ref.second_sum, ref.hidden),
            ),
        ]

    zero = chain_call(
        2,
        "layer_zero",
        dict(
            branch=branch,
            held=hidden,
            params=norm_params,
            bias_in=bias_in,
            hidden_shard=hidden_moved[0],
            attention_shard=attention_shard,
            next_cotangent=cotangent,
        ),
        dict(
            first_sum=own_kind,
            second_sum=own_kind,
            hidden=own_kind,
            mlp_input=all_kind,
            pre_gelu=gelu_kind,
            act=act_kind,
            rows=all_kind,
            hidden_full=hidden_kind,
            attention_full=attention_kind,
            moved_cotangent=low_kind,
        ),
        dict(normed=own_kind, branch_two=all_kind),
        zero_stages,
        gathers=(("hidden_shard", "hidden_full"), ("attention_shard", "attention_full")),
        swapped=(("next_cotangent", "moved_cotangent"),),
        early=((("first_sum", "mlp_input", "pre_gelu", "act", "hidden_full"), 0),),
    )

    branch, stored_one = attention(1, zero["rows"], zero["attention_full"])

    def one_stages(ref, counting):
        if counting:
            return 3
        ref.layer = 1
        return [
            dict(
                part=ref.branch,
                rows=ref.mlp_input,
                between=forward_norm(ref, ref.held, 1, 0, ref.first_sum, ref.normed),
                work=hidden_forward(ref, hidden_width),
            ),
            dict(
                part=ref.branch_two,
                rows=ref.down_full,
                between=turn_norm(ref, ref.normed, 1, 1, ref.pulled, ref.sums_two),
                work=hidden_backward(ref, hidden_width),
            ),
            dict(
                part=ref.branch_three,
                rows=ref.rows,
                between=backward_norm(ref, ref.pulled, 1, 0, ref.first_sum, ref.grad_first, ref.sums_one),
                **hidden_grads(ref, ref.grads),
            ),
        ]

    one = chain_call(
        3,
        "layer_one",
        dict(
            branch=branch,
            held=zero["hidden"],
            params=norm_params,
            bias_in=bias_in,
            hidden_shard=hidden_moved[1],
            cotangent=zero["moved_cotangent"],
        ),
        dict(
            encoded=low_kind,
            grad_first=own_kind,
            sums_one=sum_kind,
            sums_two=sum_kind,
            in_sums=in_sum_kind,
            rows=all_kind,
            grads=hidden_kind,
        ),
        dict(
            mlp_input=all_kind,
            act=act_kind,
            down_full=all_kind,
            pre_low=act_kind,
            first_sum=own_kind,
            normed=own_kind,
            pulled=own_kind,
            pre_gelu=gelu_kind,
            hidden_full=hidden_kind,
            branch_two=all_kind,
            branch_three=all_kind,
        ),
        one_stages,
        gathers=(("hidden_shard", "hidden_full"),),
        early=((("encoded",), 1),),
    )
    branch, pieces, qkv_sums_one = attention_back(stored_one, one["rows"])

    def back_stages(ref, counting):
        if counting:
            return 2
        return [
            dict(
                part=ref.branch,
                rows=ref.down_full,
                between=backward_norm(ref, ref.held, 0, 1, ref.second_sum, ref.pulled, ref.sums_two),
                work=hidden_backward(ref, hidden_width),
            ),
            dict(
                part=ref.branch_three,
                rows=ref.rows,
                between=backward_norm(ref, ref.pulled, 0, 0, ref.first_sum, ref.grad_first, ref.sums_one),
                **hidden_grads(ref, ref.grads),
            ),
        ]

    back = chain_call(
        4,
        "layer_back",
        dict(
            branch=branch,
            held=one["grad_first"],
            params=norm_params,
            first_sum=zero["first_sum"],
            second_sum=zero["second_sum"],
            pre_gelu=zero["pre_gelu"],
            hidden_full=zero["hidden_full"],
            mlp_input=zero["mlp_input"],
            act=zero["act"],
            grad_w_qkv=pieces[0],
            grad_w_out=pieces[1],
            grad_hidden=one["grads"],
            own_encoded=one["encoded"],
        ),
        dict(
            grad_first=own_kind,
            sums_one=sum_kind,
            sums_two=sum_kind,
            in_sums=in_sum_kind,
            rows=all_kind,
            moved_grads=grads_kind,
            grads=hidden_kind,
            encoded=low_kind,
        ),
        dict(later_grads=grads_kind, down_full=all_kind, pre_low=act_kind, pulled=own_kind, branch_three=all_kind),
        back_stages,
        scatters=((("grad_w_qkv", "grad_w_out", "grad_hidden"), "later_grads"),),
        swapped=(("own_encoded", "encoded"),),
        swapped_after=(("later_grads", "moved_grads"),),
        late=("pre_gelu", "hidden_full", "mlp_input", "act"),
        pace=2,
    )
    branch, pieces, qkv_sums_zero = attention_back(stored_zero, back["rows"])
    g_tokens, grads_zero, small = end(
        branch,
        back["grad_first"],
        (*pieces, back["grads"]),
        (
            (back["sums_one"], back["sums_two"], qkv_sums_zero, back["in_sums"]),
            (one["sums_one"], one["sums_two"], qkv_sums_one, one["in_sums"]),
        ),
    )
    return (
        back["encoded"],
        g_tokens,
        *finish(small, grads_zero, back["moved_grads"], col_width),
    )


def solution(mesh):
    placed = (
        P(("dp", "tensor"), None),
        P("dp", None),
        P(None, "dp", None, "tensor"),
        P(),
        P(None, "tensor", "dp"),
        P(),
        P(None, "dp", "tensor"),
        P(),
        P(None, "tensor", "dp"),
        P(),
        P(),
        P(),
        P(("dp", "tensor"), None),
    )
    return jax.shard_map(
        shards,
        mesh=mesh,
        in_specs=placed,
        out_specs=(
            P(("dp", "tensor"), None),
            P(("dp", "tensor"), None),
            P(None, "dp", None, "tensor"),
            P(),
            P(None, "tensor", "dp"),
            P(),
            P(None, "dp", "tensor"),
            P(),
            P(None, "tensor", "dp"),
            P(),
            P(),
            P(),
        ),
        check_vma=False,
    )
```

time: 400 us -> 348 us (0.87)
  matrix products: 83 us -> 0 us
  Pallas kernels: 257 us -> 311 us
  other arithmetic: 18.4 us -> 5.78 us
  local copies, waits for them, and re-layouts: 32.3 us -> 24.6 us
    dot_general x36 -> x0, matrix products: 83 us -> none  [the longest x2 16.3 us: shards(): pre_gelu = jnp.dot(mlp_input, full_in, preferred_element_type=F32) + bias_in]
    pallas_call x9 -> x10, Pallas kernels: 257 us -> 311 us  [the longest x3 195 us: chain_call(): pl.pallas_call(kernel, out_shape=tuple(shapes), in_specs=[HBM if key in (...]
    concatenate x5 -> x1, local copies, waits for them, and re-layouts: 9.62 us -> 0.01 us  [shards(): jnp.concatenate([bias_qv[:, 0], jnp.zeros((layers, col_width), F32), bias...]
    slice x21 -> x1, local copies, waits for them, and re-layouts: 7.53 us -> 0.01 us  [attention(): qkv, context, lse, branch = attend(lengths, rows, full, bias_qkv[at:at + 1])]
    unnamed x118 -> x49, local copies, waits for them, and re-layouts: 10.9 us -> 17.9 us
    convert_element_type x10 -> x3, other arithmetic: 8.34 us -> 2.65 us  [the longest x1 1.36 us: shards(): norm_params = jnp.concatenate([b_out, b_down, ln_gain.reshape(4, width),...]
where the time goes in v1:
time: 348 us; the launch traced here: 343 us
  Pallas kernels  311 us (89%)
  local copies, waits for them, and re-layouts  24.6 us (7%)
  other arithmetic  5.78 us (2%)
    pallas_call x3, Pallas kernels, chain_call(): pl.pallas_call(kernel, out_shape=tuple(shapes), in_specs=[HBM if key in (...  195 us
    pallas_call x1, Pallas kernels, end(): pl.pallas_call(end_kernel, out_shape=(shape((rows, width), BF16), shape((...  39.9 us
    pallas_call x1, Pallas kernels, start(): pl.pallas_call(start_kernel, out_shape=(shape((8, rows, width), BF16), sh...  29.8 us
    pallas_call x2, Pallas kernels, attend_back(): pl.pallas_call(attend_back_kernel, out_shape=(shape((depth, 3 * width), B...  28.1 us
    unnamed x49, local copies, waits for them, and re-layouts  17.9 us
    pallas_call x2, Pallas kernels, attend(): pl.pallas_call(attend_kernel, out_shape=(shape((total, 3 * width), BF16),...  17.7 us

profile of v1, /device:TPU:1, one launch (start us, length us, event | category | flops | bytes accessed | tf_op | source)
XLA Modules:
  0.0 342.7 jit_solution(2161983079846243806)
XLA Ops:
  0.6 0.0 copy-start
  0.7 0.7 constant_dynamic-slice_fusion
  1.4 1.3 dynamic-slice_convert_fusion.refs_3_
  2.7 1.3 pad.4.lengths
  4.0 0.7 reshape.79
  4.7 0.7 reshape.80
  5.4 1.4 maximum_convert_fusion.refs_2_
  6.8 0.0 copy-done
  6.8 1.4 pad_maximum_fusion.1.attention
  8.2 1.7 pad_maximum_fusion.hidden
  9.9 29.8 %start.1 = (bf16[8,128,1024]{2,1,0:T(8,128)(2,1)}, bf16[16,64,512]{2,1,0:T(8,128)(2,1)}, bf16[64,512]{1,0:T(8,128)(2,1)}, bf16[2,64,1024]{2,1,0:T(8,128)(2,1)}, s32[8,128]{1,0:T(8,128)}) custom-call(bf16[128,1024]{1,0:T(8,128)(2,1)} %tokens.1, bf16[2,64,512]{2,1,0:T(8,128)(2,1)} %pad_maximum_fusion.1.attention, bf16[2,64,1024]{2,1,0:T(8,128)(2,1)} %pad_maximum_fusion.hidden, ...), custom_call_target="tpu_custom_call" | custom-call | tf_op jit(solution)/shard_map/start/pallas_call | solution.py:619
  39.7 1.7 dynamic-slice_bitcast_fusion.refs_1_
  41.4 1.7 slice_bitcast_fusion
  43.1 1.2 copy-done.1
  44.3 0.7 copy-done.16
  45.0 8.7 %attend.2 = (bf16[1024,384]{1,0:T(8,128)(2,1)S(1)}, bf16[1024,128]{1,0:T(8,128)(2,1)S(1)}, f32[8,1024]{1,0:T(8,128)S(1)}, bf16[1024,1024]{1,0:T(8,128)(2,1)S(1)}) custom-call(s32[8,128]{1,0:T(8,128)S(1)} %copy-done.16, bf16[1024,1024]{1,0:T(8,128)(2,1)} %bitcast.43, bf16[1024,512]{1,0:T(8,128)(2,1)S(1)} %bitcast.31, f32[1,384]{1,0:T(1,128)S(1)} %get-tuple-element.157.bias), custom_call_target="tpu_custom_call" | custom-call | tf_op jit(solution)/shard_map/attend/pallas_call | solution.py:1165
  53.7 0.0 copy-start.8
  53.8 1.3 copy-done.8
  55.1 60.2 %layer_zero.1 = (f32[128,1024]{1,0:T(8,128)}, f32[128,1024]{1,0:T(8,128)}, f32[128,1024]{1,0:T(8,128)}, bf16[8,128,1024]{2,1,0:T(8,128)(2,1)}, f32[8,128,512]{2,...) custom-call(bf16[8,128,1024]{2,1,0:T(8,128)(2,1)} %bitcast.38, ...), custom_call_target="tpu_custom_call" | custom-call | tf_op jit(solution)/shard_map/layer_zero/pallas_call | solution.py:912
  115.3 0.0 copy-done.17
  115.3 0.0 copy-start.3
  115.3 1.2 copy-done.3
  116.6 8.9 %attend.3 = (bf16[1024,384]{1,0:T(8,128)(2,1)S(1)}, bf16[1024,128]{1,0:T(8,128)(2,1)S(1)}, f32[8,1024]{1,0:T(8,128)S(1)}, bf16[1024,1024]{1,0:T(8,128)(2,1)S(1)}) custom-call(s32[8,128]{1,0:T(8,128)S(1)} %copy-done.17, bf16[1024,1024]{1,0:T(8,128)(2,1)} %bitcast.45, bf16[1024,512]{1,0:T(8,128)(2,1)S(1)} %bitcast.33, f32[1,384]{1,0:T(1,128)S(1)} %get-tuple-element.156.bias), custom_call_target="tpu_custom_call" | custom-call | tf_op jit(solution)/shard_map/attend/pallas_call | solution.py:1165
  125.5 0.0 copy-start.6
  125.5 1.3 copy-done.6
  126.8 77.9 %layer_one.1 = (bf16[128,1024]{1,0:T(8,128)(2,1)}, f32[128,1024]{1,0:T(8,128)}, f32[8,1024]{1,0:T(8,128)}, f32[8,1024]{1,0:T(8,128)}, f32[8,512]{1,0:T(8,128)}, ...) custom-call(bf16[8,128,1024]{2,1,0:T(8,128)(2,1)} %bitcast.36, f32[128,1024]{1,0:T(8,128)} %get-tuple-element.80.refs_1_, ...), custom_call_target="tpu_custom_call" | custom-call | tf_op jit(solution)/shard_map/layer_one/pallas_call | solution.py:912
  204.7 14.2 %attend_back.2 = (bf16[1024,384]{1,0:T(8,128)(2,1)S(1)}, bf16[1024,128]{1,0:T(8,128)(2,1)S(1)}, bf16[1024,1024]{1,0:T(8,128)(2,1)S(1)}, f32[8,384]{1,0:T(8,128)S(1)}) custom-call(s32[8,128]{1,0:T(8,128)S(1)} %copy-done.17, bf16[1024,1024]{1,0:T(8,128)(2,1)} %bitcast.48, bf16[1024,1024]{1,0:T(8,128)(2,1)} %bitcast.46, bf16[1024,512]{1,0:T(8,128)(2,1)S(1)} %bitcast.34, ...), custom_call_target="tpu_custom_call" | custom-call | tf_op jit(solution)/shard_map/attend_back/pallas_call | solution.py:1259
  218.9 0.0 copy-start.5
  218.9 1.3 copy-done.5
  220.2 0.9 copy-done.9
  221.0 0.7 copy-done.12
  221.7 56.4 %layer_back.1 = (f32[128,1024]{1,0:T(8,128)}, f32[8,1024]{1,0:T(8,128)}, f32[8,1024]{1,0:T(8,128)}, f32[8,512]{1,0:T(8,128)}, bf16[8,128,1024]{2,1,0:T(8,128)(2,...) custom-call(bf16[8,128,1024]{2,1,0:T(8,128)(2,1)} %bitcast.35, ...), custom_call_target="tpu_custom_call" | custom-call | tf_op jit(solution)/shard_map/layer_back/pallas_call | solution.py:912
  278.2 13.9 %attend_back.3 = (bf16[1024,384]{1,0:T(8,128)(2,1)S(1)}, bf16[1024,128]{1,0:T(8,128)(2,1)S(1)}, bf16[1024,1024]{1,0:T(8,128)(2,1)S(1)}, f32[8,384]{1,0:T(8,128)S(1)}) custom-call(s32[8,128]{1,0:T(8,128)S(1)} %copy-done.17, bf16[1024,1024]{1,0:T(8,128)(2,1)} %bitcast.47, bf16[1024,1024]{1,0:T(8,128)(2,1)} %bitcast.44, bf16[1024,512]{1,0:T(8,128)(2,1)S(1)} %bitcast.32, ...), custom_call_target="tpu_custom_call" | custom-call | tf_op jit(solution)/shard_map/attend_back/pallas_call | solution.py:1259
  292.2 0.0 copy-start.7
  292.2 1.3 copy-done.7
  293.5 0.9 copy-done.10
  294.4 0.7 copy-done.13
  295.1 0.6 copy-done.19
  295.7 39.9 %end.1 = (bf16[128,1024]{1,0:T(8,128)(2,1)}, bf16[64,1536]{1,0:T(8,128)(2,1)}, f32[8,16,1024]{2,1,0:T(8,128)}) custom-call(bf16[8,128,1024]{2,1,0:T(8,128)(2,1)} %bitcast.37, f32[128,1024]{1,0:T(8,128)} %get-tuple-element.104.refs_1_, bf16[16,64,384]{2,1,0:T(8,128)(2,1)} %bitcast.40, bf16[16,64,128]{2,1,0:T(8,128)(2,1)} %bitcast.42, ...), custom_call_target="tpu_custom_call" | custom-call | tf_op jit(solution)/shard_map/end/pallas_call | solution.py:1015
  335.6 1.0 copy-done.11
  336.6 0.9 copy-done.15
  337.6 1.0 finish.1
  338.6 0.7 copy.32
  339.3 0.7 copy.33
  340.0 0.9 copy.34
  340.9 0.7 copy.41
  341.6 0.0 copy-done.21
  341.6 0.7 copy.42
  (28 shorter events, 0.1 us)
Async XLA Ops:
  0.6 6.1 %copy-start = (bf16[2,64,3,128]{3,1,2,0:T(8,128)(2,1)S(1)}, bf16[2,64,3,128]{3,1,2,0:T(8,128)(2,1)}, u32[]{:S(2)}) copy-start(bf16[2,64,3,128]{3,1,2,0:T(8,128)(2,1)} %param.15) | copy-start | bytes 294916
  43.1 1.2 copy-start.1
  44.3 0.7 copy-start.16
  53.7 1.4 copy-start.8
  55.1 60.2 %copy-start.17 = (s32[8,128]{1,0:T(8,128)S(1)}, s32[8,128]{1,0:T(8,128)}, u32[]{:S(2)}) copy-start(s32[8,128]{1,0:T(8,128)} %get-tuple-element.71.lengths) | copy-start | bytes 12292
  115.3 1.2 copy-start.3
  125.5 1.3 copy-start.6
  126.8 77.9 %copy-start.4 = (bf16[16,64,512]{2,1,0:T(8,128)(2,1)S(1)}, bf16[16,64,512]{2,1,0:T(8,128)(2,1)}, u32[]{:S(2)}) copy-start(bf16[16,64,512]{2,1,0:T(8,128)(2,1)} %get-tuple-element.78) | copy-start | bytes 3145732
  218.9 1.3 copy-start.5
  220.2 0.9 copy-start.9
  221.0 0.7 copy-start.12
  221.7 56.4 %copy-start.18 = (f32[8,384]{1,0:T(8,128)}, f32[8,384]{1,0:T(8,128)S(1)}, u32[]{:S(2)}) copy-start(f32[8,384]{1,0:T(8,128)S(1)} %get-tuple-element.114.refs_11_) | copy-start | bytes 36868
  221.7 56.5 %copy-start.2 = (bf16[16,64,512]{2,1,0:T(8,128)(2,1)S(1)}, bf16[16,64,512]{2,1,0:T(8,128)(2,1)}, u32[]{:S(2)}) copy-start(bf16[16,64,512]{2,1,0:T(8,128)(2,1)} %get-tuple-element.73) | copy-start | bytes 3145732
  292.2 1.4 copy-start.7
  293.5 0.9 copy-start.10
  294.4 0.7 copy-start.13
  295.1 0.6 copy-start.19
  295.7 39.9 %copy-start.14 = (bf16[64,1536]{1,0:T(8,128)(2,1)S(1)}, bf16[64,1536]{1,0:T(8,128)(2,1)}, u32[]{:S(2)}) copy-start(bf16[64,1536]{1,0:T(8,128)(2,1)} %get-tuple-element.119.one) | copy-start | bytes 589828
  295.7 45.2 %copy-start.20 = (bf16[128,1024]{1,0:T(8,128)(2,1)S(1)}, bf16[128,1024]{1,0:T(8,128)(2,1)}, u32[]{:S(2)}) copy-start(bf16[128,1024]{1,0:T(8,128)(2,1)} %get-tuple-element.172) | copy-start | bytes 786436
  335.6 1.0 copy-start.11
  336.6 0.9 copy-start.15
  337.6 4.0 %copy-start.21 = (bf16[128,1024]{1,0:T(8,128)(2,1)S(1)}, bf16[128,1024]{1,0:T(8,128)(2,1)}, u32[]{:S(2)}) copy-start(bf16[128,1024]{1,0:T(8,128)(2,1)} %get-tuple-element.173) | copy-start | bytes 786436

commit v2 on v1

--- a/solution.py
+++ b/solution.py
@@ -576,7 +576,8 @@
 
 
 def start_kernel(
-    tokens, attention, hidden, lengths, rows_out, weights_out, attention_out, hidden_out, lengths_out,
+    tokens, attention, hidden, lengths,
+    rows_out, own_out, weights_out, attention_out, hidden_first, hidden_later, lengths_out,
     ssend, srecv, send, recv, wsend, wrecv,
 ):
     x, y, z, core = place()
@@ -602,10 +603,12 @@
         ticks.append(None)
         next(steps, None)
         if len(ticks) == 3:
-            swaps.copy(hidden, hidden_out)
+            swaps.copy(hidden.at[0], hidden_first)
             swaps.copy(attention.at[1], attention_out)
+            swaps.copy(hidden.at[1], hidden_later)
 
     gather_all(group, rows_out, tick, arrivals)
+    own_out[...] = rows_out[core * 4 + y]
     drain(steps)
     swaps.finish(weights_move, *rows_moves)
     group.wait_sends()
@@ -620,14 +623,16 @@
         start_kernel,
         out_shape=(
             shape((8, rows, width), BF16),
+            shape((rows, width), BF16),
             shape((16, held, columns), BF16),
             shape((held, columns), BF16),
-            shape(hidden.shape, BF16),
+            shape(hidden.shape[1:], BF16),
+            shape(hidden.shape[1:], BF16),
             shape(lengths.shape, lengths.dtype),
         ),
         in_specs=[VMEM] * 4,
-        out_specs=(VMEM,) * 5,
-        scratch_shapes=sems(6) + sems(GATHER_COPIES) + sems(PLANE_GATHER_COPIES),
+        out_specs=(VMEM,) * 7,
+        scratch_shapes=sems(7) + sems(GATHER_COPIES) + sems(PLANE_GATHER_COPIES),
         compiler_params=params(0),
         name="start",
     )(tokens, attention, hidden, lengths)
@@ -1115,7 +1120,7 @@
     return jnp.where(features < DH, parts[0], parts[1])
 
 
-CHUNK = 512
+CHUNK = 1024
 
 
 def attend_kernel(lengths, rows, weights, bias, qkv_out, context_out, lse_out, branch_out, v_turned, seg_row):
@@ -1307,10 +1312,9 @@
     )
     hidden_shards = jnp.concatenate([w_in, w_down.transpose(0, 2, 1)], axis=2)
     lengths = jnp.pad(lengths, ((0, 7), (0, 128 - lengths.shape[1])))
-    rows_zero, attention_zero, attention_shard, hidden_moved, lengths = start(
+    rows_zero, hidden, attention_zero, attention_shard, hidden_zero, hidden_one, lengths = start(
         tokens, attention_shards, hidden_shards, lengths
     )
-    hidden = lax.dynamic_index_in_dim(rows_zero, column, 0, keepdims=False)
 
     norm_params = jnp.concatenate(
         [b_out, b_down, ln_gain.reshape(4, width), ln_bias.reshape(4, width)]
@@ -1371,7 +1375,7 @@
             held=hidden,
             params=norm_params,
             bias_in=bias_in,
-            hidden_shard=hidden_moved[0],
+            hidden_shard=hidden_zero,
             attention_shard=attention_shard,
             next_cotangent=cotangent,
         ),
@@ -1429,7 +1433,7 @@
             held=zero["hidden"],
             params=norm_params,
             bias_in=bias_in,
-            hidden_shard=hidden_moved[1],
+            hidden_shard=hidden_one,
             cotangent=zero["moved_cotangent"],
         ),
         dict(

time: 348 us -> 338 us (0.971)
  Pallas kernels: 311 us -> 304 us
    pallas_call x2, Pallas kernels: 28.1 us -> 22.6 us  [attend_back(): pl.pallas_call(attend_back_kernel, out_shape=(shape((depth, 3 * width), B...]
where the time goes in v2:
time: 338 us; the launch traced here: 332 us
  Pallas kernels  304 us (90%)
  local copies, waits for them, and re-layouts  21.3 us (6%)
  other arithmetic  5.78 us (2%)
    pallas_call x3, Pallas kernels, chain_call(): pl.pallas_call(kernel, out_shape=tuple(shapes), in_specs=[HBM if key in (...  195 us
    pallas_call x1, Pallas kernels, end(): pl.pallas_call(end_kernel, out_shape=(shape((rows, width), BF16), shape((...  40.9 us
    pallas_call x1, Pallas kernels, start(): pl.pallas_call(start_kernel, out_shape=(shape((8, rows, width), BF16), sh...  29.9 us
    pallas_call x2, Pallas kernels, attend_back(): pl.pallas_call(attend_back_kernel, out_shape=(shape((depth, 3 * width), B...  22.6 us
    unnamed x49, local copies, waits for them, and re-layouts  17.9 us
    pallas_call x2, Pallas kernels, attend(): pl.pallas_call(attend_kernel, out_shape=(shape((total, 3 * width), BF16),...  14.3 us

profile of v2, /device:TPU:1, one launch (start us, length us, event | category | flops | bytes accessed | tf_op | source)
XLA Modules:
  0.0 331.9 jit_solution(4643496654179878304)
XLA Ops:
  0.6 0.0 copy-start
  0.7 0.7 constant_dynamic-slice_fusion
  1.4 1.3 dynamic-slice_convert_fusion.refs_3_
  2.7 1.3 pad.4.lengths
  4.0 0.7 reshape.79
  4.7 0.7 reshape.80
  5.4 1.4 maximum_convert_fusion.refs_2_
  6.7 0.0 copy-done
  6.8 1.4 pad_maximum_fusion.1.attention
  8.2 1.7 pad_maximum_fusion.hidden
  9.9 29.9 %start.1 = (bf16[8,128,1024]{2,1,0:T(8,128)(2,1)}, bf16[128,1024]{1,0:T(8,128)(2,1)}, bf16[16,64,512]{2,1,0:T(8,128)(2,1)}, bf16[64,512]{1,0:T(8,128)(2,1)}, bf1...) custom-call(bf16[128,1024]{1,0:T(8,128)(2,1)} %tokens.1, ...), custom_call_target="tpu_custom_call" | custom-call | tf_op jit(solution)/shard_map/start/pallas_call | solution.py:622
  39.8 0.0 copy-start.1
  39.8 1.2 copy-done.1
  41.0 0.7 copy-done.16
  41.7 7.2 %attend.2 = (bf16[1024,384]{1,0:T(8,128)(2,1)S(1)}, bf16[1024,128]{1,0:T(8,128)(2,1)S(1)}, f32[8,1024]{1,0:T(8,128)S(1)}, bf16[1024,1024]{1,0:T(8,128)(2,1)S(1)}) custom-call(s32[8,128]{1,0:T(8,128)S(1)} %copy-done.16, bf16[1024,1024]{1,0:T(8,128)(2,1)} %bitcast.37, bf16[1024,512]{1,0:T(8,128)(2,1)S(1)} %bitcast.25, f32[1,384]{1,0:T(1,128)S(1)} %get-tuple-element.159.bias), custom_call_target="tpu_custom_call" | custom-call | tf_op jit(solution)/shard_map/attend/pallas_call | solution.py:1170
  48.9 0.0 copy-start.8
  48.9 1.3 copy-done.8
  50.2 60.1 %layer_zero.1 = (f32[128,1024]{1,0:T(8,128)}, f32[128,1024]{1,0:T(8,128)}, f32[128,1024]{1,0:T(8,128)}, bf16[8,128,1024]{2,1,0:T(8,128)(2,1)}, f32[8,128,512]{2,...) custom-call(bf16[8,128,1024]{2,1,0:T(8,128)(2,1)} %bitcast.32, ...), custom_call_target="tpu_custom_call" | custom-call | tf_op jit(solution)/shard_map/layer_zero/pallas_call | solution.py:917
  110.3 0.0 copy-done.17
  110.3 0.0 copy-start.3
  110.3 1.2 copy-done.3
  111.5 7.1 %attend.3 = (bf16[1024,384]{1,0:T(8,128)(2,1)S(1)}, bf16[1024,128]{1,0:T(8,128)(2,1)S(1)}, f32[8,1024]{1,0:T(8,128)S(1)}, bf16[1024,1024]{1,0:T(8,128)(2,1)S(1)}) custom-call(s32[8,128]{1,0:T(8,128)S(1)} %copy-done.17, bf16[1024,1024]{1,0:T(8,128)(2,1)} %bitcast.39, bf16[1024,512]{1,0:T(8,128)(2,1)S(1)} %bitcast.27, f32[1,384]{1,0:T(1,128)S(1)} %get-tuple-element.158.bias), custom_call_target="tpu_custom_call" | custom-call | tf_op jit(solution)/shard_map/attend/pallas_call | solution.py:1170
  118.7 0.0 copy-start.6
  118.7 1.3 copy-done.6
  120.0 78.6 %layer_one.1 = (bf16[128,1024]{1,0:T(8,128)(2,1)}, f32[128,1024]{1,0:T(8,128)}, f32[8,1024]{1,0:T(8,128)}, f32[8,1024]{1,0:T(8,128)}, f32[8,512]{1,0:T(8,128)}, ...) custom-call(bf16[8,128,1024]{2,1,0:T(8,128)(2,1)} %bitcast.30, f32[128,1024]{1,0:T(8,128)} %get-tuple-element.83.refs_1_, ...), custom_call_target="tpu_custom_call" | custom-call | tf_op jit(solution)/shard_map/layer_one/pallas_call | solution.py:917
  198.6 0.0 copy-done.4
  198.6 11.3 %attend_back.2 = (bf16[1024,384]{1,0:T(8,128)(2,1)S(1)}, bf16[1024,128]{1,0:T(8,128)(2,1)S(1)}, bf16[1024,1024]{1,0:T(8,128)(2,1)S(1)}, f32[8,384]{1,0:T(8,128)S(1)}) custom-call(s32[8,128]{1,0:T(8,128)S(1)} %copy-done.17, bf16[1024,1024]{1,0:T(8,128)(2,1)} %bitcast.42, bf16[1024,1024]{1,0:T(8,128)(2,1)} %bitcast.40, bf16[1024,512]{1,0:T(8,128)(2,1)S(1)} %bitcast.28, ...), custom_call_target="tpu_custom_call" | custom-call | tf_op jit(solution)/shard_map/attend_back/pallas_call | solution.py:1264
  209.9 0.0 copy-start.5
  209.9 1.3 copy-done.5
  211.2 0.9 copy-done.9
  212.1 0.7 copy-done.12
  212.8 56.3 %layer_back.1 = (f32[128,1024]{1,0:T(8,128)}, f32[8,1024]{1,0:T(8,128)}, f32[8,1024]{1,0:T(8,128)}, f32[8,512]{1,0:T(8,128)}, bf16[8,128,1024]{2,1,0:T(8,128)(2,...) custom-call(bf16[8,128,1024]{2,1,0:T(8,128)(2,1)} %bitcast.29, ...), custom_call_target="tpu_custom_call" | custom-call | tf_op jit(solution)/shard_map/layer_back/pallas_call | solution.py:917
  269.1 0.0 copy-done.18
  269.1 0.0 copy-done.2
  269.1 11.3 %attend_back.3 = (bf16[1024,384]{1,0:T(8,128)(2,1)S(1)}, bf16[1024,128]{1,0:T(8,128)(2,1)S(1)}, bf16[1024,1024]{1,0:T(8,128)(2,1)S(1)}, f32[8,384]{1,0:T(8,128)S(1)}) custom-call(s32[8,128]{1,0:T(8,128)S(1)} %copy-done.17, bf16[1024,1024]{1,0:T(8,128)(2,1)} %bitcast.41, bf16[1024,1024]{1,0:T(8,128)(2,1)} %bitcast.38, bf16[1024,512]{1,0:T(8,128)(2,1)S(1)} %bitcast.26, ...), custom_call_target="tpu_custom_call" | custom-call | tf_op jit(solution)/shard_map/attend_back/pallas_call | solution.py:1264
  280.5 1.3 copy-done.7
  281.8 0.9 copy-done.10
  282.7 0.7 copy-done.13
  283.4 0.6 copy-done.19
  284.0 40.9 %end.1 = (bf16[128,1024]{1,0:T(8,128)(2,1)}, bf16[64,1536]{1,0:T(8,128)(2,1)}, f32[8,16,1024]{2,1,0:T(8,128)}) custom-call(bf16[8,128,1024]{2,1,0:T(8,128)(2,1)} %bitcast.31, f32[128,1024]{1,0:T(8,128)} %get-tuple-element.108.refs_1_, bf16[16,64,384]{2,1,0:T(8,128)(2,1)} %bitcast.34, bf16[16,64,128]{2,1,0:T(8,128)(2,1)} %bitcast.36, ...), custom_call_target="tpu_custom_call" | custom-call | tf_op jit(solution)/shard_map/end/pallas_call | solution.py:1020
  325.0 1.0 copy-done.11
  326.0 0.9 copy-done.15
  326.9 1.0 finish.1
  327.9 0.7 copy.32
  328.6 0.7 copy.33
  329.3 0.9 copy.34
  330.2 0.7 copy.41
  330.9 0.7 copy.42
  (26 shorter events, 0.1 us)
Async XLA Ops:
  0.6 6.1 %copy-start = (bf16[2,64,3,128]{3,1,2,0:T(8,128)(2,1)S(1)}, bf16[2,64,3,128]{3,1,2,0:T(8,128)(2,1)}, u32[]{:S(2)}) copy-start(bf16[2,64,3,128]{3,1,2,0:T(8,128)(2,1)} %param.15) | copy-start | bytes 294916
  39.8 1.2 copy-start.1
  41.0 0.7 copy-start.16
  48.9 1.4 copy-start.8
  50.2 60.1 %copy-start.17 = (s32[8,128]{1,0:T(8,128)S(1)}, s32[8,128]{1,0:T(8,128)}, u32[]{:S(2)}) copy-start(s32[8,128]{1,0:T(8,128)} %get-tuple-element.73.lengths) | copy-start | bytes 12292
  110.3 1.2 copy-start.3
  118.7 1.3 copy-start.6
  120.0 78.6 %copy-start.4 = (bf16[16,64,512]{2,1,0:T(8,128)(2,1)S(1)}, bf16[16,64,512]{2,1,0:T(8,128)(2,1)}, u32[]{:S(2)}) copy-start(bf16[16,64,512]{2,1,0:T(8,128)(2,1)} %get-tuple-element.81) | copy-start | bytes 3145732
  209.9 1.3 copy-start.5
  211.2 0.9 copy-start.9
  212.1 0.7 copy-start.12
  212.8 56.3 %copy-start.18 = (f32[8,384]{1,0:T(8,128)}, f32[8,384]{1,0:T(8,128)S(1)}, u32[]{:S(2)}) copy-start(f32[8,384]{1,0:T(8,128)S(1)} %get-tuple-element.118.refs_11_) | copy-start | bytes 36868
  212.8 56.3 %copy-start.2 = (bf16[16,64,512]{2,1,0:T(8,128)(2,1)S(1)}, bf16[16,64,512]{2,1,0:T(8,128)(2,1)}, u32[]{:S(2)}) copy-start(bf16[16,64,512]{2,1,0:T(8,128)(2,1)} %get-tuple-element.75) | copy-start | bytes 3145732
  280.5 1.4 copy-start.7
  281.8 0.9 copy-start.10
  282.7 0.7 copy-start.13
  283.4 0.6 copy-start.19
  284.0 40.9 %copy-start.14 = (bf16[64,1536]{1,0:T(8,128)(2,1)S(1)}, bf16[64,1536]{1,0:T(8,128)(2,1)}, u32[]{:S(2)}) copy-start(bf16[64,1536]{1,0:T(8,128)(2,1)} %get-tuple-element.123.one) | copy-start | bytes 589828
  284.0 46.2 %copy-start.20 = (bf16[128,1024]{1,0:T(8,128)(2,1)S(1)}, bf16[128,1024]{1,0:T(8,128)(2,1)}, u32[]{:S(2)}) copy-start(bf16[128,1024]{1,0:T(8,128)(2,1)} %get-tuple-element.174) | copy-start | bytes 786436
  324.9 1.0 copy-start.11
  326.0 0.9 copy-start.15
  326.9 4.0 %copy-start.21 = (bf16[128,1024]{1,0:T(8,128)(2,1)S(1)}, bf16[128,1024]{1,0:T(8,128)(2,1)}, u32[]{:S(2)}) copy-start(bf16[128,1024]{1,0:T(8,128)(2,1)} %get-tuple-element.175) | copy-start | bytes 786436

commit v3 on v2

--- a/solution.py
+++ b/solution.py
@@ -576,11 +576,21 @@
 
 
 def start_kernel(
-    tokens, attention, hidden, lengths,
+    tokens, w_qkv, w_out, w_in, w_down, row_lengths, b_qv, b_out, b_in, b_down, ln_gain, ln_bias,
     rows_out, own_out, weights_out, attention_out, hidden_first, hidden_later, lengths_out,
+    norms_out, bias_in_out, bias_qkv_out, attention, hidden, lengths,
     ssend, srecv, send, recv, wsend, wrecv,
 ):
     x, y, z, core = place()
+    third, width = w_out.shape[2], w_in.shape[2]
+    for at in (0, 1):
+        for which in range(3):
+            attention[at, :, which * third : (which + 1) * third] = w_qkv[at, which]
+        attention[at, :, 3 * third :] = w_out[at]
+        hidden[at, :, :width] = w_in[at]
+        hidden[at, :, width:] = w_down[at]
+    lengths[...] = jnp.zeros_like(lengths)
+    lengths[0:1, 0:4] = row_lengths[...]
     greet_with_partner(neighbours())
     plane, group, swaps = Copies(wsend, wrecv), Copies(send, recv), Swaps(ssend, srecv)
     there = block_of(core * 2 + lax.rem(x, 2), z)
@@ -609,15 +619,31 @@
 
     gather_all(group, rows_out, tick, arrivals)
     own_out[...] = rows_out[core * 4 + y]
+    norms_out[0:2] = b_out[...].astype(F32)
+    norms_out[2:4] = b_down[...].astype(F32)
+    for at in (0, 1):
+        norms_out[4 + 2 * at : 6 + 2 * at] = ln_gain[at].astype(F32)
+        norms_out[8 + 2 * at : 10 + 2 * at] = ln_bias[at].astype(F32)
+    column = core * 4 + y
+    own_in = pl.ds(pl.multiple_of(column * width, width), width)
+    own_qv = pl.ds(pl.multiple_of(column * third, third), third)
+    bias_in_out[...] = b_in[:, own_in].astype(F32)
+    for at in (0, 1):
+        row = b_qv[at, :, own_qv].astype(F32)
+        bias_qkv_out[at : at + 1, :third] = row[0:1]
+        bias_qkv_out[at : at + 1, third : 2 * third] = jnp.zeros((1, third), F32)
+        bias_qkv_out[at : at + 1, 2 * third :] = row[1:2]
     drain(steps)
     swaps.finish(weights_move, *rows_moves)
     group.wait_sends()
     plane.wait_sends()
 
 
-def start(tokens, attention, hidden, lengths):
+def start(tokens, w_qkv, w_out, w_in, w_down, *others):
     rows, width = tokens.shape
-    _, held, columns = attention.shape
+    layers, held, hidden_width = w_in.shape
+    third = w_out.shape[2]
+    columns, hidden_columns = 4 * third, 2 * hidden_width
     shape = jax.ShapeDtypeStruct
     return pl.pallas_call(
         start_kernel,
@@ -626,16 +652,26 @@
             shape((rows, width), BF16),
             shape((16, held, columns), BF16),
             shape((held, columns), BF16),
-            shape(hidden.shape[1:], BF16),
-            shape(hidden.shape[1:], BF16),
-            shape(lengths.shape, lengths.dtype),
+            shape((held, hidden_columns), BF16),
+            shape((held, hidden_columns), BF16),
+            shape((8, 128), jnp.int32),
+            shape((12, width), F32),
+            shape((2, hidden_width), F32),
+            shape((2, 3 * third), F32),
         ),
-        in_specs=[VMEM] * 4,
-        out_specs=(VMEM,) * 7,
-        scratch_shapes=sems(7) + sems(GATHER_COPIES) + sems(PLANE_GATHER_COPIES),
+        in_specs=[VMEM] * 12,
+        out_specs=(VMEM,) * 10,
+        scratch_shapes=[
+            pltpu.VMEM((layers, held, columns), BF16),
+            pltpu.VMEM((layers, held, hidden_columns), BF16),
+            pltpu.VMEM((8, 128), jnp.int32),
+        ]
+        + sems(7)
+        + sems(GATHER_COPIES)
+        + sems(PLANE_GATHER_COPIES),
         compiler_params=params(0),
         name="start",
-    )(tokens, attention, hidden, lengths)
+    )(tokens, w_qkv, w_out, w_in, w_down, *others)
 
 
 def normed_parts(stream):
@@ -1046,18 +1082,20 @@
 
 
 def finish_kernel(
-    small, zero, one,
-    g_qkv, g_b_qv, g_out, g_b_out, g_in, g_b_in, g_down, g_b_down, g_gain, g_shift,
+    small, zero, one, encoded, rows,
+    encoded_out, rows_out, g_qkv, g_b_qv, g_out, g_b_out, g_in, g_b_in, g_down, g_b_down, g_gain, g_shift,
 ):
-    third, hidden_width = g_out.shape[1], g_in.shape[2]
+    third, hidden_width = g_out.shape[2], g_in.shape[2]
     cut = 4 * third
+    encoded_out[...] = encoded[...]
+    rows_out[...] = rows[...]
     for at, grads in enumerate((zero, one)):
         for which in range(3):
             columns = slice(which * third, (which + 1) * third)
-            g_qkv[at, :, which] = grads[:, columns].astype(F32)
-        g_out[at] = grads[:, 3 * third : cut].astype(F32).T
+            g_qkv[at, which] = grads[:, columns].astype(F32)
+        g_out[at] = grads[:, 3 * third : cut].astype(F32)
         g_in[at] = grads[:, cut : cut + hidden_width].astype(F32)
-        g_down[at] = grads[:, cut + hidden_width :].astype(F32).T
+        g_down[at] = grads[:, cut + hidden_width :].astype(F32)
         rows = jnp.sum(small[:, at * 8 : at * 8 + 8], axis=0)
         g_gain[at, 0:1], g_shift[at, 0:1], g_b_out[at : at + 1] = rows[0:1], rows[1:2], rows[2:3]
         g_gain[at, 1:2], g_shift[at, 1:2], g_b_down[at : at + 1] = rows[3:4], rows[4:5], rows[5:6]
@@ -1070,29 +1108,31 @@
             g_b_in[at : at + 1, columns] = row[:, 2 * third : 2 * third + hidden_width]
 
 
-def finish(small, zero, one, third):
+def finish(small, zero, one, encoded, rows, third):
     kept, hidden_width = zero.shape[0], (zero.shape[1] - 4 * third) // 2
     width = small.shape[2]
     shapes = (
-        (2, kept, 3, third),
+        (2, 3, kept, third),
         (2, 2, width),
-        (2, third, kept),
+        (2, kept, third),
         (2, width),
         (2, kept, hidden_width),
         (2, 8 * hidden_width),
-        (2, hidden_width, kept),
+        (2, kept, hidden_width),
         (2, width),
         (2, 2, width),
         (2, 2, width),
     )
+    outs = [jax.ShapeDtypeStruct(encoded.shape, BF16)] * 2
+    outs += [jax.ShapeDtypeStruct(shape, F32) for shape in shapes]
     return pl.pallas_call(
         finish_kernel,
-        out_shape=tuple(jax.ShapeDtypeStruct(shape, F32) for shape in shapes),
-        in_specs=[VMEM] * 3,
-        out_specs=(VMEM,) * len(shapes),
+        out_shape=tuple(outs),
+        in_specs=[VMEM] * 5,
+        out_specs=(VMEM,) * len(outs),
         compiler_params=pltpu.CompilerParams(vmem_limit_bytes=48 * 2**20),
         name="finish",
-    )(small, zero, one)
+    )(small, zero, one, encoded, rows)
 
 
 HEAD_SCALE = DH ** (-0.5)
@@ -1178,7 +1218,7 @@
         in_specs=[pl.BlockSpec(memory_space=pltpu.SMEM)] + [VMEM] * 3,
         out_specs=(VMEM,) * 4,
         scratch_shapes=[pltpu.VMEM((width, total), BF16), pltpu.VMEM((8, total), jnp.int32)],
-        compiler_params=pltpu.CompilerParams(vmem_limit_bytes=48 * 2**20),
+        compiler_params=pltpu.CompilerParams(vmem_limit_bytes=60 * 2**20),
         name="attend",
     )(lengths, rows, weights, bias)
 
@@ -1279,7 +1319,7 @@
             pltpu.VMEM((total, width), F32),
             pltpu.VMEM((8, total), jnp.int32),
         ],
-        compiler_params=pltpu.CompilerParams(vmem_limit_bytes=48 * 2**20),
+        compiler_params=pltpu.CompilerParams(vmem_limit_bytes=60 * 2**20),
         name="attend_back",
     )(lengths, grad_rows, rows, weights, qkv, context, lse)
 
@@ -1299,30 +1339,18 @@
     ln_bias,
     cotangent,
 ):
-    x, y, z, core = place()
-    column = core * 4 + y
     own_rows, width = tokens.shape
     total_rows = own_rows * 8
     layers, kept = w_qkv.shape[:2]
     col_width = w_qkv.shape[3]
     hidden_width = w_in.shape[2]
 
-    attention_shards = jnp.concatenate(
-        [w_qkv.reshape(layers, kept, 3 * col_width), w_out.transpose(0, 2, 1)], axis=2
-    )
-    hidden_shards = jnp.concatenate([w_in, w_down.transpose(0, 2, 1)], axis=2)
-    lengths = jnp.pad(lengths, ((0, 7), (0, 128 - lengths.shape[1])))
-    rows_zero, hidden, attention_zero, attention_shard, hidden_zero, hidden_one, lengths = start(
-        tokens, attention_shards, hidden_shards, lengths
-    )
-
-    norm_params = jnp.concatenate(
-        [b_out, b_down, ln_gain.reshape(4, width), ln_bias.reshape(4, width)]
-    ).astype(F32)
-    bias_in = lax.dynamic_slice_in_dim(b_in, column * hidden_width, hidden_width, 1).astype(F32)
-    bias_qv = lax.dynamic_slice_in_dim(b_qv, column * col_width, col_width, 2).astype(F32)
-    bias_qkv = jnp.concatenate(
-        [bias_qv[:, 0], jnp.zeros((layers, col_width), F32), bias_qv[:, 1]], axis=1
+    (
+        rows_zero, hidden, attention_zero, attention_shard, hidden_zero, hidden_one, lengths,
+        norm_params, bias_in, bias_qkv,
+    ) = start(
+        tokens, w_qkv.transpose(0, 2, 1, 3), w_out.transpose(0, 2, 1), w_in,
+        w_down.transpose(0, 2, 1), lengths, b_qv, b_out, b_in, b_down, ln_gain, ln_bias,
     )
 
     own_kind = ((own_rows, width), F32)
@@ -1528,10 +1556,22 @@
             (one["sums_one"], one["sums_two"], qkv_sums_one, one["in_sums"]),
         ),
     )
+    (
+        encoded, g_tokens, g_qkv, g_b_qv, g_out, g_b_out, g_in, g_b_in, g_down, g_b_down, g_gain, g_shift,
+    ) = finish(small, grads_zero, back["moved_grads"], back["encoded"], g_tokens, col_width)
     return (
-        back["encoded"],
+        encoded,
         g_tokens,
-        *finish(small, grads_zero, back["moved_grads"], col_width),
+        g_qkv.transpose(0, 2, 1, 3),
+        g_b_qv,
+        g_out.transpose(0, 2, 1),
+        g_b_out,
+        g_in,
+        g_b_in,
+        g_down.transpose(0, 2, 1),
+        g_b_down,
+        g_gain,
+        g_shift,
     )
 
 

time: 338 us -> 321 us (0.950)
  local copies, waits for them, and re-layouts: 21.3 us -> 4.25 us
  Pallas kernels: 304 us -> 310 us
  other arithmetic: 5.78 us -> 0 us
    unnamed x49 -> x10, local copies, waits for them, and re-layouts: 17.9 us -> 2.92 us
    pallas_call x2, Pallas kernels: 22.6 us -> 26.6 us  [attend_back(): pl.pallas_call(attend_back_kernel, out_shape=(shape((depth, 3 * width), B...]
where the time goes in v3:
time: 321 us; the launch traced here: 315 us
  Pallas kernels  310 us (97%)
  local copies, waits for them, and re-layouts  4.25 us (1%)
    pallas_call x3, Pallas kernels, chain_call(): pl.pallas_call(kernel, out_shape=tuple(shapes), in_specs=[HBM if key in (...  195 us
    pallas_call x1, Pallas kernels, end(): pl.pallas_call(end_kernel, out_shape=(shape((rows, width), BF16), shape((...  39.8 us
    pallas_call x1, Pallas kernels, start(): pl.pallas_call(start_kernel, out_shape=(shape((8, rows, width), BF16), sh...  30.2 us
    pallas_call x2, Pallas kernels, attend_back(): pl.pallas_call(attend_back_kernel, out_shape=(shape((depth, 3 * width), B...  26.6 us
    pallas_call x2, Pallas kernels, attend(): pl.pallas_call(attend_kernel, out_shape=(shape((total, 3 * width), BF16),...  17.6 us

profile of v3, /device:TPU:1, one launch (start us, length us, event | category | flops | bytes accessed | tf_op | source)
XLA Modules:
  0.0 315.2 jit_solution(5521195479810116279)
XLA Ops:
  0.6 30.2 %start.1 = (bf16[8,128,1024]{2,1,0:T(8,128)(2,1)}, bf16[128,1024]{1,0:T(8,128)(2,1)}, bf16[16,64,512]{2,1,0:T(8,128)(2,1)}, bf16[64,512]{1,0:T(8,128)(2,1)}, bf1...) custom-call(bf16[128,1024]{1,0:T(8,128)(2,1)} %tokens.1, ...), custom_call_target="tpu_custom_call" | custom-call | tf_op jit(solution)/shard_map/start/pallas_call | solution.py:648
  30.9 1.3 fusion
  32.2 8.8 %attend.2 = (bf16[1024,384]{1,0:T(8,128)(2,1)}, bf16[1024,128]{1,0:T(8,128)(2,1)}, f32[8,1024]{1,0:T(8,128)}, bf16[1024,1024]{1,0:T(8,128)(2,1)}) custom-call(s32[8,128]{1,0:T(8,128)} %get-tuple-element.78.lengths, bf16[1024,1024]{1,0:T(8,128)(2,1)} %bitcast.20, bf16[1024,512]{1,0:T(8,128)(2,1)} %bitcast.24, f32[1,384]{1,0:T(1,128)} %get-tuple-element.145.bias), custom_call_target="tpu_custom_call" | custom-call | tf_op jit(solution)/shard_map/attend/pallas_call | solution.py:1210
  41.0 60.2 %layer_zero.1 = (f32[128,1024]{1,0:T(8,128)}, f32[128,1024]{1,0:T(8,128)}, f32[128,1024]{1,0:T(8,128)}, bf16[8,128,1024]{2,1,0:T(8,128)(2,1)}, f32[8,128,512]{2,...) custom-call(bf16[8,128,1024]{2,1,0:T(8,128)(2,1)} %bitcast.31, ...), custom_call_target="tpu_custom_call" | custom-call | tf_op jit(solution)/shard_map/layer_zero/pallas_call | solution.py:953
  101.2 8.8 %attend.3 = (bf16[1024,384]{1,0:T(8,128)(2,1)}, bf16[1024,128]{1,0:T(8,128)(2,1)}, f32[8,1024]{1,0:T(8,128)}, bf16[1024,1024]{1,0:T(8,128)(2,1)}) custom-call(s32[8,128]{1,0:T(8,128)} %get-tuple-element.78.lengths, bf16[1024,1024]{1,0:T(8,128)(2,1)} %bitcast.22, bf16[1024,512]{1,0:T(8,128)(2,1)} %bitcast.26, f32[1,384]{1,0:T(1,128)} %get-tuple-element.144.bias), custom_call_target="tpu_custom_call" | custom-call | tf_op jit(solution)/shard_map/attend/pallas_call | solution.py:1210
  110.0 77.9 %layer_one.1 = (bf16[128,1024]{1,0:T(8,128)(2,1)}, f32[128,1024]{1,0:T(8,128)}, f32[8,1024]{1,0:T(8,128)}, f32[8,1024]{1,0:T(8,128)}, f32[8,512]{1,0:T(8,128)}, ...) custom-call(bf16[8,128,1024]{2,1,0:T(8,128)(2,1)} %bitcast.29, f32[128,1024]{1,0:T(8,128)} %get-tuple-element.91.refs_1_, ...), custom_call_target="tpu_custom_call" | custom-call | tf_op jit(solution)/shard_map/layer_one/pallas_call | solution.py:953
  188.0 13.4 %attend_back.2 = (bf16[1024,384]{1,0:T(8,128)(2,1)}, bf16[1024,128]{1,0:T(8,128)(2,1)}, bf16[1024,1024]{1,0:T(8,128)(2,1)}, f32[8,384]{1,0:T(8,128)}) custom-call(s32[8,128]{1,0:T(8,128)} %get-tuple-element.78.lengths, bf16[1024,1024]{1,0:T(8,128)(2,1)} %bitcast.33, bf16[1024,1024]{1,0:T(8,128)(2,1)} %bitcast.23, bf16[1024,512]{1,0:T(8,128)(2,1)} %bitcast.27, ...), custom_call_target="tpu_custom_call" | custom-call | tf_op jit(solution)/shard_map/attend_back/pallas_call | solution.py:1304
  201.3 56.5 %layer_back.1 = (f32[128,1024]{1,0:T(8,128)}, f32[8,1024]{1,0:T(8,128)}, f32[8,1024]{1,0:T(8,128)}, f32[8,512]{1,0:T(8,128)}, bf16[8,128,1024]{2,1,0:T(8,128)(2,...) custom-call(bf16[8,128,1024]{2,1,0:T(8,128)(2,1)} %bitcast.28, ...), custom_call_target="tpu_custom_call" | custom-call | tf_op jit(solution)/shard_map/layer_back/pallas_call | solution.py:953
  257.8 13.2 %attend_back.3 = (bf16[1024,384]{1,0:T(8,128)(2,1)}, bf16[1024,128]{1,0:T(8,128)(2,1)}, bf16[1024,1024]{1,0:T(8,128)(2,1)}, f32[8,384]{1,0:T(8,128)}) custom-call(s32[8,128]{1,0:T(8,128)} %get-tuple-element.78.lengths, bf16[1024,1024]{1,0:T(8,128)(2,1)} %bitcast.32, bf16[1024,1024]{1,0:T(8,128)(2,1)} %bitcast.21, bf16[1024,512]{1,0:T(8,128)(2,1)} %bitcast.25, ...), custom_call_target="tpu_custom_call" | custom-call | tf_op jit(solution)/shard_map/attend_back/pallas_call | solution.py:1304
  271.0 0.0 copy-start.1
  271.0 0.0 copy-start.3
  271.0 39.8 %end.1 = (bf16[128,1024]{1,0:T(8,128)(2,1)}, bf16[64,1536]{1,0:T(8,128)(2,1)}, f32[8,16,1024]{2,1,0:T(8,128)}) custom-call(bf16[8,128,1024]{2,1,0:T(8,128)(2,1)} %bitcast.30, f32[128,1024]{1,0:T(8,128)} %get-tuple-element.115.refs_1_, bf16[16,64,384]{2,1,0:T(8,128)(2,1)} %bitcast.35, bf16[16,64,128]{2,1,0:T(8,128)(2,1)} %bitcast.37, ...), custom_call_target="tpu_custom_call" | custom-call | tf_op jit(solution)/shard_map/end/pallas_call | solution.py:1056
  310.9 0.0 copy-done.1
  310.9 0.0 copy-done.3
  310.9 0.0 copy-start
  310.9 1.0 copy-done
  312.0 0.0 copy-start.2
  312.0 0.9 copy-done.2
  312.9 0.0 copy-start.4
  312.9 0.9 copy-done.4
  313.8 1.2 finish.1
Async XLA Ops:
  271.0 39.9 %copy-start.1 = (bf16[128,1024]{1,0:T(8,128)(2,1)S(1)}, bf16[128,1024]{1,0:T(8,128)(2,1)}, u32[]{:S(2)}) copy-start(bf16[128,1024]{1,0:T(8,128)(2,1)} %get-tuple-element.130.encoded) | copy-start | bytes 786436
  271.0 39.9 %copy-start.3 = (bf16[64,1536]{1,0:T(8,128)(2,1)S(1)}, bf16[64,1536]{1,0:T(8,128)(2,1)}, u32[]{:S(2)}) copy-start(bf16[64,1536]{1,0:T(8,128)(2,1)} %get-tuple-element.129.one) | copy-start | bytes 589828
  310.9 1.0 copy-start
  312.0 0.9 copy-start.2
  312.9 0.9 copy-start.4

commit v4 on v3

--- a/solution.py
+++ b/solution.py
@@ -1130,7 +1130,7 @@
         out_shape=tuple(outs),
         in_specs=[VMEM] * 5,
         out_specs=(VMEM,) * len(outs),
-        compiler_params=pltpu.CompilerParams(vmem_limit_bytes=48 * 2**20),
+        compiler_params=pltpu.CompilerParams(vmem_limit_bytes=60 * 2**20),
         name="finish",
     )(small, zero, one, encoded, rows)
 
@@ -1163,7 +1163,7 @@
 CHUNK = 1024
 
 
-def attend_kernel(lengths, rows, weights, bias, qkv_out, context_out, lse_out, branch_out, v_turned, seg_row):
+def attend_kernel(layer, lengths, rows, weights, bias, qkv_out, context_out, lse_out, branch_out, v_turned, seg_row):
     total, width = rows.shape[0], context_out.shape[1]
     column, row = segment_parts(lengths, total)
     seg_row[...] = jnp.broadcast_to(row, seg_row.shape)
@@ -1175,7 +1175,7 @@
     def _(at):
         r = chunk(at)
         qkv = jnp.dot(rows[r], weights[:, : 3 * width], preferred_element_type=F32)
-        qkv_out[r] = (qkv + bias[0:1]).astype(BF16)
+        qkv_out[r] = (qkv + bias[layer : layer + 1]).astype(BF16)
 
     keys = qkv_out[:, width : 2 * width]
     v_turned[...] = qkv_out[:, 2 * width :].astype(F32).T.astype(BF16)
@@ -1204,11 +1204,11 @@
         branch_out[r] = branch.astype(BF16)
 
 
-def attend(lengths, rows, weights, bias):
+def attend(layer, lengths, rows, weights, bias):
     total, width = rows.shape[0], weights.shape[1] // 4
     shape = jax.ShapeDtypeStruct
     return pl.pallas_call(
-        attend_kernel,
+        functools.partial(attend_kernel, layer),
         out_shape=(
             shape((total, 3 * width), BF16),
             shape((total, width), BF16),
@@ -1366,7 +1366,7 @@
 
     def attention(at, rows, full):
         rows, full = rows.reshape(total_rows, width), full.reshape(width, 4 * col_width)
-        qkv, context, lse, branch = attend(lengths, rows, full, bias_qkv[at : at + 1])
+        qkv, context, lse, branch = attend(at, lengths, rows, full, bias_qkv)
         return branch.reshape(all_kind[0]), (rows, full, qkv, context, lse)
 
     def attention_back(stored, rows):

time: 321 us -> 318 us (level)
  local copies, waits for them, and re-layouts: 4.25 us -> 0 us
where the time goes in v4:
time: 318 us; the launch traced here: 313 us
  Pallas kernels  312 us (98%)
    pallas_call x3, Pallas kernels, chain_call(): pl.pallas_call(kernel, out_shape=tuple(shapes), in_specs=[HBM if key in (...  195 us
    pallas_call x1, Pallas kernels, end(): pl.pallas_call(end_kernel, out_shape=(shape((rows, width), BF16), shape((...  40.3 us
    pallas_call x1, Pallas kernels, start(): pl.pallas_call(start_kernel, out_shape=(shape((8, rows, width), BF16), sh...  30.2 us
    pallas_call x2, Pallas kernels, attend_back(): pl.pallas_call(attend_back_kernel, out_shape=(shape((depth, 3 * width), B...  26.8 us
    pallas_call x2, Pallas kernels, attend(): pl.pallas_call(functools.partial(attend_kernel, layer), out_shape=(shape(...  17.6 us

profile of v4, /device:TPU:1, one launch (start us, length us, event | category | flops | bytes accessed | tf_op | source)
XLA Modules:
  0.0 312.7 jit_solution(6915586802367115489)
XLA Ops:
  0.6 30.2 %start.1 = (bf16[8,128,1024]{2,1,0:T(8,128)(2,1)}, bf16[128,1024]{1,0:T(8,128)(2,1)}, bf16[16,64,512]{2,1,0:T(8,128)(2,1)}, bf16[64,512]{1,0:T(8,128)(2,1)}, bf1...) custom-call(bf16[128,1024]{1,0:T(8,128)(2,1)} %tokens.1, ...), custom_call_target="tpu_custom_call" | custom-call | tf_op jit(solution)/shard_map/start/pallas_call | solution.py:648
  30.8 8.9 %attend.2 = (bf16[1024,384]{1,0:T(8,128)(2,1)}, bf16[1024,128]{1,0:T(8,128)(2,1)}, f32[8,1024]{1,0:T(8,128)}, bf16[1024,1024]{1,0:T(8,128)(2,1)}) custom-call(s32[8,128]{1,0:T(8,128)} %get-tuple-element.78.lengths, bf16[1024,1024]{1,0:T(8,128)(2,1)} %bitcast.20, bf16[1024,512]{1,0:T(8,128)(2,1)} %bitcast.24, f32[2,384]{1,0:T(2,128)} %get-tuple-element.81.bias), custom_call_target="tpu_custom_call" | custom-call | tf_op jit(solution)/shard_map/attend/pallas_call | solution.py:1210
  39.7 60.1 %layer_zero.1 = (f32[128,1024]{1,0:T(8,128)}, f32[128,1024]{1,0:T(8,128)}, f32[128,1024]{1,0:T(8,128)}, bf16[8,128,1024]{2,1,0:T(8,128)(2,1)}, f32[8,128,512]{2,...) custom-call(bf16[8,128,1024]{2,1,0:T(8,128)(2,1)} %bitcast.31, ...), custom_call_target="tpu_custom_call" | custom-call | tf_op jit(solution)/shard_map/layer_zero/pallas_call | solution.py:953
  99.8 8.8 %attend.3 = (bf16[1024,384]{1,0:T(8,128)(2,1)}, bf16[1024,128]{1,0:T(8,128)(2,1)}, f32[8,1024]{1,0:T(8,128)}, bf16[1024,1024]{1,0:T(8,128)(2,1)}) custom-call(s32[8,128]{1,0:T(8,128)} %get-tuple-element.78.lengths, bf16[1024,1024]{1,0:T(8,128)(2,1)} %bitcast.22, bf16[1024,512]{1,0:T(8,128)(2,1)} %bitcast.26, f32[2,384]{1,0:T(2,128)} %get-tuple-element.81.bias), custom_call_target="tpu_custom_call" | custom-call | tf_op jit(solution)/shard_map/attend/pallas_call | solution.py:1210
  108.6 78.0 %layer_one.1 = (bf16[128,1024]{1,0:T(8,128)(2,1)}, f32[128,1024]{1,0:T(8,128)}, f32[8,1024]{1,0:T(8,128)}, f32[8,1024]{1,0:T(8,128)}, f32[8,512]{1,0:T(8,128)}, ...) custom-call(bf16[8,128,1024]{2,1,0:T(8,128)(2,1)} %bitcast.29, f32[128,1024]{1,0:T(8,128)} %get-tuple-element.91.refs_1_, ...), custom_call_target="tpu_custom_call" | custom-call | tf_op jit(solution)/shard_map/layer_one/pallas_call | solution.py:953
  186.6 13.6 %attend_back.2 = (bf16[1024,384]{1,0:T(8,128)(2,1)}, bf16[1024,128]{1,0:T(8,128)(2,1)}, bf16[1024,1024]{1,0:T(8,128)(2,1)}, f32[8,384]{1,0:T(8,128)}) custom-call(s32[8,128]{1,0:T(8,128)} %get-tuple-element.78.lengths, bf16[1024,1024]{1,0:T(8,128)(2,1)} %bitcast.33, bf16[1024,1024]{1,0:T(8,128)(2,1)} %bitcast.23, bf16[1024,512]{1,0:T(8,128)(2,1)} %bitcast.27, ...), custom_call_target="tpu_custom_call" | custom-call | tf_op jit(solution)/shard_map/attend_back/pallas_call | solution.py:1304
  200.1 56.4 %layer_back.1 = (f32[128,1024]{1,0:T(8,128)}, f32[8,1024]{1,0:T(8,128)}, f32[8,1024]{1,0:T(8,128)}, f32[8,512]{1,0:T(8,128)}, bf16[8,128,1024]{2,1,0:T(8,128)(2,...) custom-call(bf16[8,128,1024]{2,1,0:T(8,128)(2,1)} %bitcast.28, ...), custom_call_target="tpu_custom_call" | custom-call | tf_op jit(solution)/shard_map/layer_back/pallas_call | solution.py:953
  256.6 13.2 %attend_back.3 = (bf16[1024,384]{1,0:T(8,128)(2,1)}, bf16[1024,128]{1,0:T(8,128)(2,1)}, bf16[1024,1024]{1,0:T(8,128)(2,1)}, f32[8,384]{1,0:T(8,128)}) custom-call(s32[8,128]{1,0:T(8,128)} %get-tuple-element.78.lengths, bf16[1024,1024]{1,0:T(8,128)(2,1)} %bitcast.32, bf16[1024,1024]{1,0:T(8,128)(2,1)} %bitcast.21, bf16[1024,512]{1,0:T(8,128)(2,1)} %bitcast.25, ...), custom_call_target="tpu_custom_call" | custom-call | tf_op jit(solution)/shard_map/attend_back/pallas_call | solution.py:1304
  269.8 40.3 %end.1 = (bf16[128,1024]{1,0:T(8,128)(2,1)}, bf16[64,1536]{1,0:T(8,128)(2,1)}, f32[8,16,1024]{2,1,0:T(8,128)}) custom-call(bf16[8,128,1024]{2,1,0:T(8,128)(2,1)} %bitcast.30, f32[128,1024]{1,0:T(8,128)} %get-tuple-element.115.refs_1_, bf16[16,64,384]{2,1,0:T(8,128)(2,1)} %bitcast.35, bf16[16,64,128]{2,1,0:T(8,128)(2,1)} %bitcast.37, ...), custom_call_target="tpu_custom_call" | custom-call | tf_op jit(solution)/shard_map/end/pallas_call | solution.py:1056
  310.0 2.5 finish.1
